TPU v7x, 512 devices: a whole 4x8x8 slice. The times are simulated.
512 devices in a mesh: seq: 64 (over y, x, core), head: 8 (over z).
Axes of the slice: x: 4, y: 8, z: 8, core: 2. Of those that a mesh axis runs over, the one named last changes fastest.
Arguments:
- queries: bfloat16 [8192, 4096], P('seq', 'head'), may hold values from -300 to 300
- keyvals: bfloat16 [8192, 8, 128], P('seq', 'head'), may hold values from -6 to 6
- out_proj: bfloat16 [4096, 2880], P('head'), may hold values from -0.09375 to 0.09375
- residual: bfloat16 [8192, 2880], P(('seq', 'head')), may hold values from -60 to 60
- norm_gain: float32 [2880], replicated, may hold values from 0.1 to 1.9
- route_ids: int32 [8192, 4], P('seq'), may hold values from 0 to 31, as said below
- route_weights: bfloat16 [8192, 4], P('seq'), may hold values from 0.049804688 to 0.5
- expert_in: bfloat16 [64, 1440, 3072], P('seq', None, 'head'), may hold values from -0.109375 to 0.109375
- expert_out: bfloat16 [64, 1536, 1440], P('seq', 'head'), may hold values from -0.15625 to 0.15625
Outputs:
- stream: bfloat16 [8192, 2880], P(('seq', 'head'))
- expert_sum: bfloat16 [8192, 2880], P(('seq', 'head'))
Inputs may be any that keep to these rules, and one draw needn't show every extreme that they name: `route_ids`: each row names 4 different experts. In each aligned block of 16 rows, one expert, the same in every block, is named by exactly 3 rows, and every other expert by at most 3 rows; the other experts' counts within a block differ by at most one.
All inputs are finite; a program needn't handle non-finite values.
Results may differ from a plain program's by a relative error of at most 0.035.
Values may be sent and summed in bfloat16 or wider, within the bound.
A program may use at most 64 MiB of HBM per device.

v0:
```python
import jax
import jax.numpy as jnp
from jax import lax
from jax.sharding import PartitionSpec as P

TOP = 4
ATTEND_SPAN = 128


def shifted(block, axis, distance):
    devices = range(lax.axis_size(axis))
    route = [(i - distance, i) for i in devices if i - distance in devices]
    return lax.ppermute(block, axis, route)


def partner(value, axis, stride):
    mask = 2**stride
    pairs = [(source, source ^ mask) for source in range(lax.axis_size(axis))]
    return lax.ppermute(value, axis, pairs)


def normalize(hidden, norm_gain):
    mean_square = jnp.mean(hidden * hidden, axis=-1, keepdims=True)
    return (hidden * lax.rsqrt(mean_square + 1e-05) * norm_gain).astype(jnp.bfloat16)


def attend(queries, keyvals, seq_at):
    tok_rows = queries.shape[0]
    kv_heads = keyvals.shape[1]
    head_dim = keyvals.shape[2] // 2
    query_group = queries.shape[1] // head_dim // kv_heads
    previous = shifted(keyvals, "seq", 1)
    joined = jnp.concatenate([previous, keyvals], axis=0)
    tile_block_count = tok_rows // ATTEND_SPAN
    key_tiles_list = jnp.concatenate(
        [
            joined[:tok_rows].reshape(tile_block_count, ATTEND_SPAN, kv_heads, 2 * head_dim),
            keyvals.reshape(tile_block_count, ATTEND_SPAN, kv_heads, 2 * head_dim),
        ],
        axis=1,
    )
    query_tiles_list = queries.reshape(
        tile_block_count, ATTEND_SPAN, kv_heads, query_group, head_dim
    )
    scores = jnp.einsum(
        "bqkgd,bjkd->bkgqj",
        query_tiles_list,
        key_tiles_list[..., :head_dim],
        preferred_element_type=jnp.float32,
    ) * head_dim ** (-0.5)
    query_pos = jnp.arange(ATTEND_SPAN, dtype=jnp.int32)[:, None]
    key_pos = jnp.arange(2 * ATTEND_SPAN, dtype=jnp.int32)[None, :]
    first_key = (
        seq_at * tok_rows
        + jnp.arange(tile_block_count, dtype=jnp.int32) * ATTEND_SPAN
        - ATTEND_SPAN
    )
    allowed = (
        (key_pos > query_pos)
        & (key_pos <= query_pos + ATTEND_SPAN)
        & (first_key[:, None, None] + key_pos[None] >= 0)
    )
    scores = jnp.where(allowed[:, None, None], scores, -1e30)
    largest = jnp.max(scores, axis=-1, keepdims=True)
    exponent = jnp.exp(scores - largest)
    attention_weights = (exponent / jnp.sum(exponent, axis=-1, keepdims=True)).astype(jnp.bfloat16)
    mixed_vals = jnp.einsum(
        "bkgqj,bjkd->bqkgd",
        attention_weights,
        key_tiles_list[..., head_dim:],
        preferred_element_type=jnp.float32,
    )
    return mixed_vals.astype(jnp.bfloat16).reshape(tok_rows, queries.shape[1])


def halves_of(padded, pick_rows, expert_count, slot_count, half_width):
    lower_half = padded[:, :half_width][pick_rows].reshape(expert_count, slot_count, half_width)
    upper_half = padded[:, half_width:][pick_rows].reshape(expert_count, slot_count, half_width)
    return jnp.stack([lower_half, upper_half], axis=1).reshape(
        2 * expert_count, slot_count, half_width
    )


def per_device(
    queries, keyvals, out_proj, residual, norm_gain, route_ids, route_weights, expert_in, expert_out
):
    head_count = lax.axis_size("head")
    seq_count = lax.axis_size("seq")
    head_at = lax.axis_index("head")
    seq_at = lax.axis_index("seq")
    tok_rows = queries.shape[0]
    own_rows = tok_rows // head_count
    model_width = residual.shape[1]
    half_width = model_width // 2
    expert_count = seq_count // 2
    capacity = max(2, 12 * tok_rows // (seq_count * head_count))
    slot_count = head_count * capacity
    attended = attend(queries, keyvals, seq_at)
    block_ids = route_ids.reshape(head_count, own_rows * TOP)
    one_hot = (block_ids[..., None] == jnp.arange(expert_count, dtype=jnp.int32)).astype(jnp.int32)
    earlier = jnp.sum((jnp.cumsum(one_hot, axis=1) - one_hot) * one_hot, axis=-1)
    slot_flat = (jnp.arange(head_count, dtype=jnp.int32)[:, None] * capacity + earlier).reshape(-1)
    expert_of = route_ids.reshape(-1)
    partial_value = jnp.dot(attended, out_proj, preferred_element_type=jnp.float32)
    placed = lax.dynamic_update_slice(
        jnp.zeros((tok_rows, model_width), jnp.float32),
        residual.astype(jnp.float32),
        (head_at * own_rows, 0),
    )
    hidden_all = lax.psum((partial_value + placed).astype(jnp.bfloat16), "head").astype(jnp.float32)
    stream = lax.dynamic_slice_in_dim(hidden_all, head_at * own_rows, own_rows, 0)
    normed = normalize(hidden_all, norm_gain)
    padded = jnp.concatenate([normed, jnp.zeros((1, model_width), jnp.bfloat16)], axis=0)
    token_of = jnp.arange(tok_rows * TOP, dtype=jnp.int32) // TOP
    pick_rows = (
        jnp.full((expert_count * slot_count,), tok_rows, jnp.int32)
        .at[expert_of * slot_count + slot_flat]
        .set(token_of)
    )
    outgoing = halves_of(padded, pick_rows, expert_count, slot_count, half_width)
    arrived = lax.all_to_all(outgoing, "seq", split_axis=0, concat_axis=0, tiled=True)
    flat_in = arrived.reshape(seq_count * slot_count, half_width)
    part_own = jnp.dot(flat_in, expert_in[0], preferred_element_type=jnp.float32).astype(
        jnp.bfloat16
    )
    part_other = partner(part_own, "seq", 0)
    inner_sum = part_own.astype(jnp.float32) + part_other.astype(jnp.float32)
    hid_units = expert_out.shape[1]
    gate_in = inner_sum[:, :hid_units]
    up_in = inner_sum[:, hid_units:]
    active = ((up_in + 1.0) * gate_in * jax.nn.sigmoid(1.702 * gate_in)).astype(jnp.bfloat16)
    down_out = jnp.dot(active, expert_out[0], preferred_element_type=jnp.float32).astype(
        jnp.bfloat16
    )
    returned = lax.all_to_all(
        down_out.reshape(seq_count, slot_count, half_width),
        "seq",
        split_axis=0,
        concat_axis=0,
        tiled=True,
    )
    flat_back = returned.reshape(seq_count * slot_count, half_width)
    row_low = (2 * expert_of * slot_count + slot_flat).reshape(tok_rows, TOP)
    lower_half = jnp.einsum(
        "tk,tkd->td", route_weights, flat_back[row_low], preferred_element_type=jnp.float32
    )
    upper_half = jnp.einsum(
        "tk,tkd->td",
        route_weights,
        flat_back[row_low + slot_count],
        preferred_element_type=jnp.float32,
    )
    expert_sum = lax.psum_scatter(
        jnp.concatenate([lower_half, upper_half], axis=1).astype(jnp.bfloat16),
        "head",
        scatter_dimension=0,
        tiled=True,
    )
    return (stream.astype(jnp.bfloat16), expert_sum)


def solution(mesh):
    placed = (
        P("seq", "head"),
        P("seq", "head", None),
        P("head", None),
        P(("seq", "head"), None),
        P(),
        P("seq", None),
        P("seq", None),
        P("seq", None, "head"),
        P("seq", "head", None),
    )
    return jax.shard_map(
        per_device,
        mesh=mesh,
        in_specs=placed,
        out_specs=(P(("seq", "head"), None), P(("seq", "head"), None)),
        check_vma=False,
    )
```

profile of v0, /device:TPU:1, one launch (start us, length us, event | category | flops | bytes accessed | tf_op | source)
XLA Modules:
  0.0 453.9 jit_solution(7056087898474385601)
XLA Ops:
  8.2 4.5 collective-permute-start
  13.8 1.4 fusion.33
  17.4 2.3 copy.58
  22.6 1.6 dynamic-slice_add_fusion
  24.1 7.8 %add.140 = f32[128,2880]{0,1:T(8,128)} dynamic-update-slice(f32[128,2880]{0,1:T(8,128)} %copy-done.1, f32[16,2880]{0,1:T(8,128)} %dynamic-slice_add_fusion, s32[]{:T(128)S(6)} %select_n.34, s32[]{:T(128)} %constant.30.clone.1) | dynamic-update-slice | bytes 368644 | tf_op jit(solution)/shard_map/add | solution.py:110
  31.9 2.4 convert_element_type.51
  34.7 2.4 scatter_custom_fusion
  37.2 78.7 %all-reduce.3.cloned.1.call-done = bf16[128,2880]{0,1:T(8,128)(2,1)} async-done(((bf16[128,2880]{0,1:T(8,128)(2,1)}), bf16[128,2880]{0,1:T(8,128)(2,1)}) %all-reduce.3.cloned.1.call-update) | async-done | bytes 737296 | tf_op jit(solution)/shard_map/psum | solution.py:110
  115.8 1.5 multiply_reduce_fusion
  117.4 1.6 multiply_convert_fusion
  118.9 1.3 pad_slice_fusion.1
  120.2 1.3 copy.64
  121.6 2.1 copy.63
  123.7 3.8 gather_fusion.1
  127.5 6.9 %gather_fusion = bf16[768,1440]{1,0:T(8,128)(2,1)} fusion(bf16[129,1440]{1,0:T(8,128)(2,1)} %copy.63, s32[1024]{0:T(1024)S(1)} %pad_clamp_fusion.2), kind=kCustom, calls=%fused_computation | custom fusion | bytes 4426752 | tf_op jit(solution)/shard_map/gather | solution.py:77
  134.4 2.8 pad_maximum_fusion
  137.3 122.5 %all_to_all.10 = bf16[64,24,1440]{2,1,0:T(8,128)(2,1)S(1)} all-to-all(bf16[64,24,1440]{2,1,0:T(8,128)(2,1)S(1)} %bitcast.60), channel_id=1, replica_groups=mesh['seq'=64,'head'=8] {'seq'}, dimensions={0} | all-to-all | bytes 8847360 | tf_op jit(solution)/shard_map/all_to_all | solution.py:121
  259.7 2.1 convolution_convert_fusion.1
  261.9 2.4 collective-permute-start.1
  264.2 2.5 collective-permute-done.1
  267.1 3.4 convolution_convert_fusion
  270.5 6.7 %copy.67 = bf16[1536,1440]{1,0:T(8,128)(2,1)} copy(bf16[1536,1440]{0,1:T(8,128)(2,1)} %convolution_convert_fusion) | data formatting | bytes 8847360 | tf_op jit(solution)/shard_map/convert_element_type | solution.py:132
  277.2 6.0 %all-to-all-start.1 = ((bf16[64,24,1440]{2,1,0:T(8,128)(2,1)}), bf16[64,24,1440]{2,1,0:T(8,128)(2,1)}, u32[]{:S(2)}, u32[]{:S(2)}) async-start(bf16[64,24,1440]{2,1,0:T(8,128)(2,1)} %bitcast.59), calls=%async_computation.1 | async-start | bytes 9437184 | tf_op jit(solution)/shard_map/all_to_all | solution.py:135
  283.8 104.6 %all-to-all-done.1 = bf16[64,24,1440]{2,1,0:T(8,128)(2,1)} async-done(((bf16[64,24,1440]{2,1,0:T(8,128)(2,1)}), bf16[64,24,1440]{2,1,0:T(8,128)(2,1)}, u32[]{:S(2)}, u32[]{:S(2)}) %all-to-all-start.1) | async-done | bytes 4423712 | tf_op jit(solution)/shard_map/all_to_all | solution.py:135
  388.4 7.3 %gather_fusion.3 = bf16[512,1440]{1,0:T(8,128)(2,1)} fusion(bf16[1536,1440]{1,0:T(8,128)(2,1)} %bitcast.23, s32[1024]{0:T(1024)S(1)} %pad_clamp_fusion), kind=kCustom, calls=%fused_computation.3 | custom fusion | bytes 2951168 | tf_op jit(solution)/shard_map/gather | solution.py:150
  395.7 3.9 reshape.239
  399.6 7.3 %gather_fusion.2 = bf16[512,1440]{1,0:T(8,128)(2,1)} fusion(bf16[1536,1440]{1,0:T(8,128)(2,1)} %bitcast.23, s32[1024]{0:T(1024)S(1)} %pad_clamp_fusion.1), kind=kCustom, calls=%fused_computation.2 | custom fusion | bytes 2951168 | tf_op jit(solution)/shard_map/gather | solution.py:145
  406.9 3.9 reshape.231
  410.8 2.5 fusion.35
  415.5 2.3 dynamic-slice_convert_fusion
  417.8 2.0 copy.72
  419.8 27.2 %reduce-scatter.2.cloned.1.call-done = bf16[16,2880]{1,0:T(8,128)(2,1)} async-done(((bf16[128,2880]{1,0:T(8,128)(2,1)}), bf16[16,2880]{1,0:T(8,128)(2,1)}) %reduce-scatter.2.cloned.1.call-update) | async-done | bytes 92176 | tf_op jit(solution)/shard_map/reduce_scatter | solution.py:153
  (60 shorter events, 10.6 us)
Async XLA Ops:
  7.2 13.3 %copy-start = (bf16[512,2880]{0,1:T(8,128)(2,1)S(1)}, bf16[512,2880]{0,1:T(8,128)(2,1)}, u32[]{:S(2)}) copy-start(bf16[512,2880]{0,1:T(8,128)(2,1)} %param.11) | copy-start | bytes 8847364
  7.2 108.7 %all-reduce.3.cloned.1.call-start = ((), (), s32[]{:S(2)}) async-start(), calls=%async_computation.3 | async-start | bytes 1474560 | tf_op jit(solution)/shard_map/psum | solution.py:110
  8.2 11.4 %collective-permute-start = (bf16[128,1,128]{0,2,1:T(8,128)(2,1)S(1)}, bf16[128,1,128]{0,2,1:T(8,128)(2,1)S(1)}, u32[]{:S(2)}, u32[]{:S(2)}) collective-permute-start(bf16[128,1,128]{0,2,1:T(8,128)(2,1)S(1)} %copy.54), channel_id=1, source_target_pairs={{0,8},{8,16},{16,24},{24,32},{32,40},{40,48},{48,56},{56,64},{64,7... | collective-permute-start | bytes 98312 | tf_op jit(solution)/shard_map/ppermute | solution.py:13
  20.5 2.1 copy-start.2
  21.4 1.1 copy-start.1
  31.9 85.4 %copy-start.4 = (f32[2880]{0:T(1024)S(1)}, f32[2880]{0:T(1024)}, u32[]{:S(2)}) copy-start(f32[2880]{0:T(1024)} %param.13) | copy-start | bytes 34564
  137.2 122.5 %copy-start.6 = (bf16[1,1440,384]{2,1,0:T(8,128)(2,1)S(1)}, bf16[1,1440,384]{2,1,0:T(8,128)(2,1)}, u32[]{:S(2)}) copy-start(bf16[1,1440,384]{2,1,0:T(8,128)(2,1)} %param.16) | copy-start | bytes 3317764
  261.8 5.2 %copy-start.7 = (bf16[1,192,1440]{2,1,0:T(8,128)(2,1)S(1)}, bf16[1,192,1440]{2,1,0:T(8,128)(2,1)}, u32[]{:S(2)}) copy-start(bf16[1,192,1440]{2,1,0:T(8,128)(2,1)} %param.17) | copy-start | bytes 1658884
  261.9 4.9 %collective-permute-start.1 = (bf16[1536,384]{0,1:T(8,128)(2,1)S(1)}, bf16[1536,384]{0,1:T(8,128)(2,1)S(1)}, u32[]{:S(2)}, u32[]{:S(2)}) collective-permute-start(bf16[1536,384]{0,1:T(8,128)(2,1)S(1)} %convolution_convert_fusion.1), channel_id=1, source_target_pairs={{0,8},{8,0},{16,24},{24,16},{32,40},{40,32},{48,56},{56,48},{64,72... | collective-permute-start | bytes 3538952 | tf_op jit(solution)/shard_map/ppermute | solution.py:19
  277.2 6.2 %copy-start.5 = (bf16[128,4]{0,1:T(4,128)(2,1)S(1)}, bf16[128,4]{0,1:T(4,128)(2,1)}, u32[]{:S(2)}) copy-start(bf16[128,4]{0,1:T(4,128)(2,1)} %param.15) | copy-start | bytes 3076
  277.2 111.2 %all-to-all-start.1 = ((bf16[64,24,1440]{2,1,0:T(8,128)(2,1)}), bf16[64,24,1440]{2,1,0:T(8,128)(2,1)}, u32[]{:S(2)}, u32[]{:S(2)}) async-start(bf16[64,24,1440]{2,1,0:T(8,128)(2,1)} %bitcast.59), calls=%async_computation.1 | async-start | bytes 9437184 | tf_op jit(solution)/shard_map/all_to_all | solution.py:135
  283.1 163.9 %reduce-scatter.2.cloned.1.call-start = ((), (), s32[]{:S(2)}) async-start(), calls=%async_computation.4 | async-start | bytes 847872 | tf_op jit(solution)/shard_map/reduce_scatter | solution.py:153
  410.8 2.5 copy-start.3
Sparse Core Ops, SparseCore 0:
  34.4 81.3 all-reduce.2
  415.6 31.3 reduce-scatter.1
where the time goes:
time: 459 us; the launch traced here: 454 us
  waiting for transfers between devices  213 us (46%)
  blocking collectives  122 us (27%)
  local copies, waits for them, and re-layouts  66.9 us (15%)
  between operations  14.3 us (3%)
  other arithmetic  13.7 us (3%)
  starting transfers between devices  12.9 us (3%)
  matrix products  10.5 us (2%)
    all_to_all x1, blocking collectives, per_device(): lax.all_to_all(outgoing, 'seq', split_axis=0, concat_axis=0, tiled=True)  122 us
    all_to_all x1, waiting for transfers between devices, per_device(): lax.all_to_all(down_out.reshape(seq_count, slot_count, half_width), 'seq'...  105 us
    psum x1, waiting for transfers between devices, per_device(): lax.psum((partial_value + placed).astype(jnp.bfloat16), 'head')  78.7 us
    reduce_scatter x1, waiting for transfers between devices, per_device(): lax.psum_scatter(jnp.concatenate([lower_half, upper_half], axis=1).astype...  27.2 us
    gather x2, local copies, waits for them, and re-layouts, per_device(): flat_back[row_low]  11.2 us
    gather x2, local copies, waits for them, and re-layouts, per_device(): flat_back[row_low + slot_count]  11.2 us
  transfers between devices with their start and end apart: 5, of which 4 were waited for; matrix products, arithmetic and copies ran while one was open for 3% of the time, Pallas kernels for 0%

commit v1 on v0

v1 whole, which is shorter than its diff:
```python
import jax
import jax.numpy as jnp
from jax import lax
from jax.experimental import pallas as pl
from jax.experimental.pallas import tpu as pltpu
from jax.sharding import PartitionSpec as P

MESH = pl.DeviceIdType.MESH
BF = jnp.bfloat16
F32 = jnp.float32
I32 = jnp.int32

NS, NZ = 64, 8
NC = NS // 2
TOK, OWN, TOP = 128, 16, 4
D, HALF, CH = 2880, 1440, 12
R = 6
CAP = R // 2
MSG = 80
GS, GR = 8, 48
NR = NC * R
H = 4
SB = NR // H
GH = SB // GR
FAR = 7


def idiv(v, n):
    if n & (n - 1) == 0:
        return lax.shift_right_logical(v, jnp.full_like(v, n.bit_length() - 1))
    return ((v.astype(F32) + 0.5) * (1.0 / n)).astype(I32)


def imod(v, n):
    return v - idiv(v, n) * n


def iota(shape, dim):
    return lax.broadcasted_iota(I32, shape, dim)


def dot(a, b):
    return jnp.dot(a, b, preferred_element_type=F32)


def dot_nt(a, b):
    return lax.dot_general(a, b, (((1,), (1,)), ((), ())), preferred_element_type=F32)


def ones(cond):
    return jnp.where(cond, 1.0, 0.0).astype(BF)


def kernel(
    q_hbm, kv_hbm, wo_hbm, res_hbm, gain_hbm, info_hbm, win_hbm, wout_hbm,
    stream_ref, esum_ref,
    q_v, kv2, wo_v, res_v, gain_v, info2, win_v, wout_v,
    att_v, own_f, ps, rs, stage, xbuf, dm, cm, pm, pt,
    sb1, rb1, slots, low_own, low_oth, qs, racc, sb2, rb2, fin, fsend,
    load_sem, kv_ss, kv_rs, info_ss, info_rs, rs_ss, rs_rs, st_ss, st_rs,
    a1_ss, a1_rs, ag_ss, ag_rs, lo_ss, lo_rs, q_ss, q_rs, a2_ss, a2_rs, f_ss, f_rs,
):
    s = lax.axis_index("seq")
    z = lax.axis_index("head")
    p = lax.rem(s, 2)
    chip = lax.div(s, 2)
    other = s + 1 - 2 * p
    nxt = lax.rem(s + 1, NS)
    prv = lax.rem(s + NS - 1, NS)
    up = lax.rem(z + 1, NZ)
    dn = lax.rem(z + NZ - 1, NZ)

    loads = [
        pltpu.make_async_copy(src, dst, load_sem.at[i])
        for i, (src, dst) in enumerate(
            [
                (kv_hbm, kv2.at[1]),
                (q_hbm, q_v),
                (info_hbm.at[pl.ds(pl.multiple_of(z * OWN, OWN), OWN)], info2.at[p]),
                (wo_hbm, wo_v),
                (res_hbm, res_v),
                (gain_hbm, gain_v),
                (win_hbm.at[0], win_v),
                (wout_hbm.at[0], wout_v),
            ]
        )
    ]
    for c in loads:
        c.start()

    barrier = pltpu.get_barrier_semaphore()

    def greet(seq, head):
        pl.semaphore_signal(barrier, inc=1, device_id=(seq, head), device_id_type=MESH)

    greet(other, z)
    greet(prv, z)

    @pl.loop(1, NZ)
    def _(d):
        greet(s, lax.rem(z + d, NZ))

    @pl.loop(1, NC)
    def _(d):
        greet(lax.rem(chip + d, NC) * 2 + p, z)

    pl.semaphore_wait(barrier, 1 + 1 + (NZ - 1) + (NC - 1))

    def remote(src, dst, ss, rs_, seq, head):
        return pltpu.make_async_remote_copy(
            src_ref=src, dst_ref=dst, send_sem=ss, recv_sem=rs_,
            device_id=(seq, head), device_id_type=MESH,
        )

    loads[0].wait()
    kv_copy = remote(kv2.at[1], kv2.at[0], kv_ss, kv_rs, nxt, z)
    kv_copy.start()
    loads[2].wait()
    info_copy = remote(info2.at[p], info2.at[p], info_ss, info_rs, other, z)
    info_copy.start()
    loads[1].wait()
    kv_copy.wait_recv()

    kvf = kv2[...].reshape(2 * TOK, 128).astype(F32)
    lane = iota((2 * TOK, 128), 1)
    turned = pltpu.roll(kvf, 64, 1)
    k_even = jnp.where(lane < 64, kvf, 0.0).astype(BF)
    k_odd = jnp.where(lane >= 64, turned, 0.0).astype(BF)
    v_even = jnp.where(lane < 64, turned, 0.0).astype(BF)
    v_odd = jnp.where(lane >= 64, kvf, 0.0).astype(BF)
    qpos = iota((TOK, 2 * TOK), 0)
    kpos = iota((TOK, 2 * TOK), 1)
    allowed = (kpos > qpos) & (kpos <= qpos + TOK) & (s * TOK - TOK + kpos >= 0)
    for pair in range(4):
        qp = q_v[:, 128 * pair:128 * (pair + 1)]
        acc = None
        for kk, vv in ((k_even, v_even), (k_odd, v_odd)):
            sc = jnp.where(allowed, dot_nt(qp, kk) * 0.125, -1e30)
            ex = jnp.exp(sc - jnp.max(sc, axis=-1, keepdims=True))
            w = (ex / jnp.sum(ex, axis=-1, keepdims=True)).astype(BF)
            part = dot(w, vv)
            acc = part if acc is None else acc + part
        att_v[:, 128 * pair:128 * (pair + 1)] = acc.astype(BF)

    loads[3].wait()
    for n0 in range(0, D, 512):
        n1 = min(D, n0 + 512)
        part = dot(att_v[...], wo_v[:, n0:n1]).reshape(NZ, OWN, n1 - n0)
        own_f[:, :, n0:n1] = part
        ps[:, :, n0:n1] = part.astype(BF)

    def rs_copy(d):
        to = lax.rem(z + d, NZ)
        return remote(ps.at[to], rs.at[d - 1], rs_ss.at[d - 1], rs_rs.at[d - 1], s, to)

    for d in (4, 3, 5, 2, 6, 1, 7):
        rs_copy(d).start()

    info_copy.wait_recv()
    inf = info2[...].reshape(2 * OWN, 128)
    lanes = iota((2 * OWN, 128), 1).astype(F32)
    named = jnp.zeros((2 * OWN, 128), F32)
    weight = jnp.zeros((2 * OWN, 128), F32)
    for k in range(TOP):
        hit = inf[:, k:k + 1] == lanes
        named = named + jnp.where(hit, 1.0, 0.0)
        weight = weight + jnp.where(hit, inf[:, TOP + k:TOP + k + 1], 0.0)
    named, weight = named.astype(BF), weight.astype(BF)
    ta, tb = iota((2 * OWN, 2 * OWN), 0), iota((2 * OWN, 2 * OWN), 1)
    before = ones((tb < ta) & (idiv(tb, OWN) == idiv(ta, OWN)))
    slot = dot(before, named).astype(BF)
    ra = iota((NC * R, 128), 0)
    expand = ones(idiv(ra, R) == iota((NC * R, 128), 1))
    r_i = imod(iota((NC * R, 2 * OWN), 0), R)
    t_i = iota((NC * R, 2 * OWN), 1)
    want = r_i - idiv(r_i, CAP) * CAP
    picked = (
        (dot_nt(expand, named) > 0.5)
        & (dot_nt(expand, slot) == want.astype(F32))
        & (idiv(t_i, OWN) == idiv(r_i, CAP))
    )
    spread = ones(iota((2 * OWN, CH * 2 * OWN), 0) == imod(iota((2 * OWN, CH * 2 * OWN), 1), 2 * OWN))
    wide = dot(ones(picked), spread).astype(BF)
    m_i = iota((NC * MSG, NC * R), 0)
    rest = imod(m_i, MSG)
    rows_of = ones(
        (idiv(m_i, MSG) * R + imod(rest, R) == iota((NC * MSG, NC * R), 1)) & (rest < CH * R)
    )
    mm = iota((MSG, CH * 2 * OWN), 0)
    chunk_ok = jnp.where(idiv(mm, R) == idiv(iota((MSG, CH * 2 * OWN), 1), 2 * OWN), 1.0, 0.0)
    full = dot(rows_of, wide).reshape(NC, MSG, CH * 2 * OWN) * chunk_ok[None]
    dm[...] = full.reshape(NC * MSG, CH * 2 * OWN).astype(BF)

    def perm(shape, a_dim):
        i, j = iota(shape, a_dim), iota(shape, 1 - a_dim)
        inner = imod(j, MSG)
        return ones(
            (idiv(i, GR) == idiv(inner, R))
            & (idiv(imod(i, GR), R) == idiv(j, MSG))
            & (imod(i, R) == imod(inner, R))
            & (inner < CH * R)
        )

    pm[...] = perm((CH * GR, GS * MSG), 0)
    pt[...] = perm((GS * MSG, CH * GR), 1)

    loads[4].wait()
    loads[5].wait()
    total = res_v[...].astype(F32) + own_f[z]
    for d in (1, 7, 2, 6, 3, 5, 4):
        rs_copy(d).wait_recv()
        total = total + rs[d - 1].astype(F32)
    stream_ref[...] = total.astype(BF)
    mean_square = jnp.mean(total * total, axis=-1, keepdims=True)
    normed = (total * lax.rsqrt(mean_square + 1e-5) * gain_v[...]).astype(BF)
    for h in range(2):
        for c in range(CH):
            lo = h * HALF + c * 128
            hi = min(lo + 128, (h + 1) * HALF)
            piece = normed[:, lo:hi]
            if hi - lo < 128:
                piece = jnp.concatenate([piece, jnp.zeros((OWN, 128 - hi + lo), BF)], axis=1)
            stage[h, c] = piece
    mine = pl.ds(pl.multiple_of(p * OWN, OWN), OWN)
    st_copy = remote(stage.at[1 - p], xbuf.at[:, mine, :], st_ss, st_rs, other, z)
    st_copy.start()
    xbuf[:, mine, :] = stage[p]
    st_copy.wait_recv()

    msgs = dot(dm[...], xbuf[...].reshape(CH * 2 * OWN, 128)).astype(BF)
    sb1[...] = msgs.reshape(NC, MSG, 128)

    def a1_copy(d):
        to = lax.rem(chip + d, NC)
        return remote(sb1.at[to], rb1.at[chip], a1_ss.at[to], a1_rs.at[chip], to * 2 + p, z)

    @pl.loop(1, NC)
    def _(d):
        a1_copy(d).start()

    rb1[chip] = sb1[chip]

    def a1_wait(src):
        @pl.when(src != chip)
        def _():
            remote(sb1.at[src], rb1.at[src], a1_ss.at[src], a1_rs.at[src], src * 2 + p, z).wait_recv()

    far_from = 3 + 3 * p
    far_to = lax.rem(z + 1 + (NZ - 2) * p, NZ)
    far_back = lax.rem(z + NZ - 1 + 2 * p, NZ)

    def rows(h):
        return pl.ds(h * SB, SB)

    def ag_copy(src, dst, h, head):
        return remote(
            slots.at[src, rows(h)], slots.at[dst, rows(h)],
            ag_ss.at[dst, h], ag_rs.at[dst, h], s, head,
        )

    def lo_copy(slot_at, h):
        return remote(
            low_own.at[slot_at, rows(h)], low_oth.at[slot_at, rows(h)],
            lo_ss.at[slot_at, h], lo_rs.at[slot_at, h], other, z,
        )

    def low(slot_at, h):
        low_own[slot_at, rows(h)] = dot(slots[slot_at, rows(h)], win_v[...]).astype(BF)
        lo_copy(slot_at, h).start()

    for h in range(H):
        for g in range(h * GH, (h + 1) * GH):
            for i in range(GS):
                a1_wait(g * GS + i)
            got = dot(pm[...], rb1[GS * g:GS * (g + 1)].reshape(GS * MSG, 128)).astype(BF)
            for c in range(CH):
                width = min(128, HALF - 128 * c)
                slots[0, GR * g:GR * (g + 1), 128 * c:128 * c + width] = got[GR * c:GR * (c + 1), :width]
        ag_copy(0, 1, h, up).start()
        ag_copy(0, 4, h, dn).start()
    loads[6].wait()
    for h in range(H):
        low(0, h)

    e_l = iota((2 * OWN, NC * R), 1)
    r_l = imod(e_l, R)
    back = ones(iota((128, NC * R), 0) == idiv(iota((128, NC * R), 1), R))
    take = (dot(slot, back) == (r_l - idiv(r_l, CAP) * CAP).astype(F32)) & (
        idiv(iota((2 * OWN, NC * R), 0), OWN) == idiv(r_l, CAP)
    )
    w_t = jnp.where(take, dot(weight, back), 0.0).astype(BF)
    spread_t = ones(iota((CH * 2 * OWN, 2 * OWN), 1) == imod(iota((CH * 2 * OWN, 2 * OWN), 0), 2 * OWN))
    tall = dot(spread_t, w_t).astype(BF)
    m_l = iota((NC * R, NC * MSG), 1)
    rest_l = imod(m_l, MSG)
    cols_of = ones(
        (idiv(m_l, MSG) * R + imod(rest_l, R) == iota((NC * R, NC * MSG), 0)) & (rest_l < CH * R)
    )
    full_t = dot(tall, cols_of)
    c_l = idiv(imod(iota((CH * 2 * OWN, NC * MSG), 1), MSG), R)
    cm[...] = jnp.where(c_l == idiv(iota((CH * 2 * OWN, NC * MSG), 0), 2 * OWN), full_t, 0.0).astype(BF)

    for k in (1, 2, 3):
        for h in range(H):
            ag_copy(0, k, h, up).wait_recv()
            if k < 3:
                ag_copy(k, k + 1, h, up).start()
            ag_copy(0, k + 3, h, dn).wait_recv()
            if k < 3:
                ag_copy(k + 3, k + 4, h, dn).start()
            else:
                ag_copy(far_from, FAR, h, far_to).start()
            low(k, h)
            low(k + 3, h)
    loads[7].wait()
    for h in range(H):
        ag_copy(far_from, FAR, h, far_to).wait_recv()
        low(FAR, h)

    def expert(slot_at, h):
        lo_copy(slot_at, h).wait_recv()
        inner = low_own[slot_at, rows(h)].astype(F32) + low_oth[slot_at, rows(h)].astype(F32)
        gate, upv = inner[:, :192], inner[:, 192:]
        active = ((upv + 1.0) * gate * jax.nn.sigmoid(1.702 * gate)).astype(BF)
        return dot(active, wout_v[...])

    def q_copy(slot_at, dst, h, head):
        return remote(
            qs.at[slot_at, rows(h)], racc.at[dst, rows(h)],
            q_ss.at[slot_at, h], q_rs.at[dst, h], s, head,
        )

    for h in range(H):
        qs[FAR, rows(h)] = expert(FAR, h).astype(BF)
        q_copy(FAR, FAR, h, far_back).start()
    for h in range(H):
        below, above = expert(3, h), expert(6, h)
        q_copy(FAR, FAR, h, far_back).wait_recv()
        got = racc[FAR, rows(h)].astype(F32)
        qs[3, rows(h)] = (below + jnp.where(p == 0, got, 0.0)).astype(BF)
        q_copy(3, 2, h, dn).start()
        qs[6, rows(h)] = (above + jnp.where(p == 0, 0.0, got)).astype(BF)
        q_copy(6, 5, h, up).start()
    for k in (2, 1):
        for h in range(H):
            below, above = expert(k, h), expert(k + 3, h)
            q_copy(k, k, h, dn).wait_recv()
            qs[k, rows(h)] = (below + racc[k, rows(h)].astype(F32)).astype(BF)
            q_copy(k, k - 1, h, dn).start()
            q_copy(k + 3, k + 3, h, up).wait_recv()
            qs[k + 3, rows(h)] = (above + racc[k + 3, rows(h)].astype(F32)).astype(BF)
            q_copy(k + 3, k + 2, h, up).start()

    def a2_copy(to):
        return remote(sb2.at[to], rb2.at[chip], a2_ss.at[to], a2_rs.at[chip], to * 2 + p, z)

    for h in range(H):
        value = expert(0, h)
        q_copy(0, 0, h, dn).wait_recv()
        q_copy(0, 3, h, up).wait_recv()
        value = (value + racc[0, rows(h)].astype(F32) + racc[3, rows(h)].astype(F32)).astype(BF)
        for i in range(GH):
            g = h * GH + i
            part = value[GR * i:GR * (i + 1)]
            pieces = [part[:, 128 * c:128 * (c + 1)] for c in range(CH - 1)]
            last = part[:, 128 * (CH - 1):]
            pieces.append(jnp.concatenate([last, jnp.zeros((GR, 128 * CH - HALF), BF)], axis=1))
            out = dot(pt[...], jnp.concatenate(pieces, axis=0)).astype(BF)
            sb2[GS * g:GS * (g + 1)] = out.reshape(GS, MSG, 128)

            @pl.loop(0, GS)
            def _(j):
                to = g * GS + j

                @pl.when(to != chip)
                def _():
                    a2_copy(to).start()

    rb2[chip] = sb2[chip]

    @pl.loop(0, NC)
    def _(src):
        @pl.when(src != chip)
        def _():
            remote(sb2.at[src], rb2.at[src], a2_ss.at[src], a2_rs.at[src], src * 2 + p, z).wait_recv()

    out = dot(cm[...], rb2[...].reshape(NC * MSG, 128)).astype(BF).reshape(CH, 2 * OWN, 128)
    cm_out = xbuf
    cm_out[...] = out
    theirs = pl.ds(pl.multiple_of((1 - p) * OWN, OWN), OWN)
    fsend[...] = cm_out[:, theirs, :]
    f_copy = remote(fsend, fin.at[p], f_ss, f_rs, other, z)
    f_copy.start()
    fin[p] = cm_out[:, mine, :]
    f_copy.wait_recv()
    esum_ref[...] = jnp.concatenate(
        [fin[h, c][:, :min(128, HALF - 128 * c)] for h in range(2) for c in range(CH)], axis=1
    )

    kv_copy.wait_send()
    info_copy.wait_send()
    st_copy.wait_send()
    f_copy.wait_send()
    for d in range(1, NZ):
        rs_copy(d).wait_send()

    @pl.loop(1, NC)
    def _(d):
        a1_copy(d).wait_send()
        a2_copy(lax.rem(chip + d, NC)).wait_send()

    for slot_at in range(8):
        for h in range(H):
            lo_copy(slot_at, h).wait_send()
            if slot_at:
                ag_copy(0, slot_at, h, up).wait_send()
                q_copy(slot_at, slot_at, h, up).wait_send()


def per_device(q, kv, wo, res, gain, ids, weights, w_in, w_out):
    info = jnp.concatenate([ids.astype(F32), weights.astype(F32), jnp.zeros((TOK, 128 - 2 * TOP), F32)], axis=1)
    vm = pltpu.VMEM
    dma = pltpu.SemaphoreType.DMA
    scratch = [
        vm((TOK, 512), BF), vm((2, TOK, 128), BF), vm((512, D), BF), vm((OWN, D), BF), vm((1, D), F32),
        vm((2, OWN, 128), F32), vm((HALF, 384), BF), vm((192, HALF), BF),
        vm((TOK, 512), BF), vm((NZ, OWN, D), F32), vm((NZ, OWN, D), BF), vm((NZ - 1, OWN, D), BF),
        vm((2, CH, OWN, 128), BF), vm((CH, 2 * OWN, 128), BF),
        vm((NC * MSG, CH * 2 * OWN), BF), vm((CH * 2 * OWN, NC * MSG), BF),
        vm((CH * GR, GS * MSG), BF), vm((GS * MSG, CH * GR), BF),
        vm((NC, MSG, 128), BF), vm((NC, MSG, 128), BF),
        vm((8, NR, HALF), BF), vm((8, NR, 384), BF), vm((8, NR, 384), BF),
        vm((8, NR, HALF), BF), vm((8, NR, HALF), BF),
        vm((NC, MSG, 128), BF), vm((NC, MSG, 128), BF),
        vm((2, CH, OWN, 128), BF), vm((CH, OWN, 128), BF),
        dma((8,)), dma, dma, dma, dma, dma((NZ - 1,)), dma((NZ - 1,)), dma, dma,
        dma((NC,)), dma((NC,)), dma((8, H)), dma((8, H)), dma((8, H)), dma((8, H)),
        dma((8, H)), dma((8, H)), dma((NC,)), dma((NC,)), dma, dma,
    ]
    return pl.pallas_call(
        kernel,
        out_shape=(jax.ShapeDtypeStruct((OWN, D), BF), jax.ShapeDtypeStruct((OWN, D), BF)),
        in_specs=[pl.BlockSpec(memory_space=pl.ANY)] * 8,
        out_specs=(pl.BlockSpec(memory_space=vm), pl.BlockSpec(memory_space=vm)),
        scratch_shapes=scratch,
        compiler_params=pltpu.CompilerParams(
            collective_id=0, has_side_effects=True, vmem_limit_bytes=58 * 1024 * 1024
        ),
        cost_estimate=pl.CostEstimate(flops=4_000_000_000, bytes_accessed=8_000_000, transcendentals=300_000),
    )(q, kv.reshape(TOK, 128), wo, res, gain.reshape(1, D), info, w_in, w_out)


def solution(mesh):
    placed = (
        P("seq", "head"), P("seq", "head", None), P("head", None), P(("seq", "head"), None), P(),
        P("seq", None), P("seq", None), P("seq", None, "head"), P("seq", "head", None),
    )
    return jax.shard_map(
        per_device, mesh=mesh, in_specs=placed,
        out_specs=(P(("seq", "head"), None), P(("seq", "head"), None)), check_vma=False,
    )
```

time: 459 us -> 185 us (0.40)
  the two profiles are of different devices: /device:TPU:1 before, /device:TPU:57 now
where the time goes in v1:
time: 185 us
  Pallas kernels  173 us (94%)
  local copies, waits for them, and re-layouts  9.93 us (5%)
    pallas_call x1, Pallas kernels, per_device(): pl.pallas_call(kernel, out_shape=(jax.ShapeDtypeStruct((OWN, D), BF), jax...  173 us
    unnamed x3, local copies, waits for them, and re-layouts  7.64 us

profile of v1, /device:TPU:57, one launch (start us, length us, event | category | flops | bytes accessed | tf_op | source)
XLA Modules:
  0.0 185.1 jit_solution(3323584091559318199)
XLA Ops:
  0.6 0.1 pad.2.clone
  0.7 0.7 convert_element_type.6
  1.4 1.3 reshape.11.gain_hbm
  2.7 0.1 copy.11
  2.8 0.8 copy.12
  3.6 0.7 maximum_maximum_fusion.info_hbm
  4.3 4.6 %copy.13.wo_hbm = bf16[512,2880]{1,0:T(8,128)(2,1)} copy(bf16[512,2880]{0,1:T(8,128)(2,1)} %param.11) | data formatting | bytes 5898240 | tf_op args[2]
  8.9 173.1 %shard_map.104 = (bf16[16,2880]{1,0:T(8,128)(2,1)}, bf16[16,2880]{1,0:T(8,128)(2,1)}) custom-call(bf16[128,512]{1,0:T(8,128)(2,1)} %q_hbm.1, bf16[128,128]{1,0:T(8,128)(2,1)} %bitcast.1, bf16[512,2880]{1,0:T(8,128)(2,1)} %copy.13.wo_hbm, bf16[16,2880]{1,0:T(8,128)(2,1)} %res_hbm.1, f32[1,2880]{1,0:T(1,128)} %reshape.11.gain_hbm, ...), custom_call_target="tpu_custom_call" | custom-call | flops 4000000000 | bytes 8000000 | tf_op jit(solution)/shard_map/pallas_call | solution.py:440
  182.0 1.5 copy.16
  183.6 1.5 copy.17
  (1 shorter events, 0.0 us)

commit v2 on v1

--- a/solution.py
+++ b/solution.py
@@ -14,15 +14,19 @@
 NC = NS // 2
 TOK, OWN, TOP = 128, 16, 4
 D, HALF, CH = 2880, 1440, 12
-R = 6
+NX, NY = 4, 8
+R = 4
 CAP = R // 2
-MSG = 80
-GS, GR = 8, 48
+MSG = 48
+GS, GR = 4, 16
 NR = NC * R
-H = 4
+H = 2
 SB = NR // H
 GH = SB // GR
 FAR = 7
+OV = 8
+OM = 32
+OB = CH * OWN
 
 
 def idiv(v, n):
@@ -52,18 +56,22 @@
 
 
 def kernel(
-    q_hbm, kv_hbm, wo_hbm, res_hbm, gain_hbm, info_hbm, win_hbm, wout_hbm,
+    q_hbm, kv_hbm, wo_hbm, res_hbm, gain_hbm, ids_hbm, rw_hbm, win_hbm, wout_hbm,
     stream_ref, esum_ref,
-    q_v, kv2, wo_v, res_v, gain_v, info2, win_v, wout_v,
+    q_v, kv2, wo_v, res_v, gain_v, ids_v, rw_v, both, info2, win_v, wout_v,
     att_v, own_f, ps, rs, stage, xbuf, dm, cm, pm, pt,
     sb1, rb1, slots, low_own, low_oth, qs, racc, sb2, rb2, fin, fsend,
+    om, co, p2, p2t, osend, oz, ox, obuf, oret, osel, oyr, ozs, ozr,
     load_sem, kv_ss, kv_rs, info_ss, info_rs, rs_ss, rs_rs, st_ss, st_rs,
     a1_ss, a1_rs, ag_ss, ag_rs, lo_ss, lo_rs, q_ss, q_rs, a2_ss, a2_rs, f_ss, f_rs,
+    oz_ss, oz_rs, oy_ss, oy_rs, ox_ss, ox_rs, or_ss, or_rs, oyr_ss, oyr_rs, ozr_ss, ozr_rs,
 ):
     s = lax.axis_index("seq")
     z = lax.axis_index("head")
     p = lax.rem(s, 2)
     chip = lax.div(s, 2)
+    x = lax.rem(chip, NX)
+    y = lax.div(chip, NX)
     other = s + 1 - 2 * p
     nxt = lax.rem(s + 1, NS)
     prv = lax.rem(s + NS - 1, NS)
@@ -76,12 +84,13 @@
             [
                 (kv_hbm, kv2.at[1]),
                 (q_hbm, q_v),
-                (info_hbm.at[pl.ds(pl.multiple_of(z * OWN, OWN), OWN)], info2.at[p]),
+                (ids_hbm, ids_v),
                 (wo_hbm, wo_v),
                 (res_hbm, res_v),
                 (gain_hbm, gain_v),
                 (win_hbm.at[0], win_v),
                 (wout_hbm.at[0], wout_v),
+                (rw_hbm, rw_v),
             ]
         )
     ]
@@ -116,6 +125,11 @@
     kv_copy = remote(kv2.at[1], kv2.at[0], kv_ss, kv_rs, nxt, z)
     kv_copy.start()
     loads[2].wait()
+    loads[8].wait()
+    both[0:TOP] = ids_v[...].astype(F32)
+    both[TOP:] = rw_v[...].astype(F32)
+    chosen = ones(iota((OWN, TOK), 1) == iota((OWN, TOK), 0) + z * OWN)
+    info2[p, :, 0:2 * TOP] = dot_nt(chosen, both[...].astype(BF))
     info_copy = remote(info2.at[p], info2.at[p], info_ss, info_rs, other, z)
     info_copy.start()
     loads[1].wait()
@@ -145,7 +159,7 @@
     loads[3].wait()
     for n0 in range(0, D, 512):
         n1 = min(D, n0 + 512)
-        part = dot(att_v[...], wo_v[:, n0:n1]).reshape(NZ, OWN, n1 - n0)
+        part = dot_nt(att_v[...], wo_v[n0:n1]).reshape(NZ, OWN, n1 - n0)
         own_f[:, :, n0:n1] = part
         ps[:, :, n0:n1] = part.astype(BF)
 
@@ -191,6 +205,29 @@
     full = dot(rows_of, wide).reshape(NC, MSG, CH * 2 * OWN) * chunk_ok[None]
     dm[...] = full.reshape(NC * MSG, CH * 2 * OWN).astype(BF)
 
+    third = jnp.where((named > 0.5) & (slot > 1.5), 1.0, 0.0)
+    third_row = dot_nt(jnp.ones((8, 128), BF), third.astype(BF))[0:1]
+    third_wide = dot(jnp.broadcast_to(third_row, (8, 2 * OWN)).astype(BF), spread)[0:1]
+    o_m, o_q = iota((OM, CH * 2 * OWN), 0), iota((OM, CH * 2 * OWN), 1)
+    o_ok = (idiv(o_m, 2) == idiv(o_q, 2 * OWN)) & (imod(o_m, 2) == imod(idiv(o_q, OWN), 2))
+    om[...] = jnp.where(o_ok, third_wide, 0.0).astype(BF)
+    hot = jnp.max(third, axis=0, keepdims=True)
+    e_row = iota((1, 128), 1)
+    hot_x = jnp.sum(hot * imod(e_row, NX).astype(F32), axis=1, keepdims=True)
+    hot_y = jnp.sum(hot * idiv(e_row, NX).astype(F32), axis=1, keepdims=True)
+
+    def perm2(shape, a_dim):
+        i, j = iota(shape, a_dim), iota(shape, 1 - a_dim)
+        inner = imod(j, OM)
+        return ones(
+            (idiv(i, OWN) == idiv(inner, 2))
+            & (idiv(imod(i, OWN), 2) == idiv(j, OM))
+            & (imod(i, 2) == imod(inner, 2))
+        )
+
+    p2[...] = perm2((OB, NZ * OM), 0)
+    p2t[...] = perm2((NZ * OM, OB), 1)
+
     def perm(shape, a_dim):
         i, j = iota(shape, a_dim), iota(shape, 1 - a_dim)
         inner = imod(j, MSG)
@@ -212,7 +249,7 @@
         total = total + rs[d - 1].astype(F32)
     stream_ref[...] = total.astype(BF)
     mean_square = jnp.mean(total * total, axis=-1, keepdims=True)
-    normed = (total * lax.rsqrt(mean_square + 1e-5) * gain_v[...]).astype(BF)
+    normed = (total * lax.rsqrt(mean_square + 1e-5) * gain_v[...].reshape(1, D)).astype(BF)
     for h in range(2):
         for c in range(CH):
             lo = h * HALF + c * 128
@@ -227,6 +264,18 @@
     xbuf[:, mine, :] = stage[p]
     st_copy.wait_recv()
 
+    osend[...] = dot(om[...], xbuf[...].reshape(CH * 2 * OWN, 128)).astype(BF)
+
+    def oz_copy(d):
+        return remote(osend, oz.at[z], oz_ss.at[d - 1], oz_rs.at[z], s, lax.rem(z + d, NZ))
+
+    for d in range(1, NZ):
+        oz_copy(d).start()
+    oz[z] = osend[...]
+
+    def at(y_, x_):
+        return (y_ * NX + x_) * 2 + p
+
     msgs = dot(dm[...], xbuf[...].reshape(CH * 2 * OWN, 128)).astype(BF)
     sb1[...] = msgs.reshape(NC, MSG, 128)
 
@@ -278,6 +327,18 @@
                 slots[0, GR * g:GR * (g + 1), 128 * c:128 * c + width] = got[GR * c:GR * (c + 1), :width]
         ag_copy(0, 1, h, up).start()
         ag_copy(0, 4, h, dn).start()
+    for d in range(1, NZ):
+        from_z = lax.rem(z + d, NZ)
+        remote(osend, oz.at[from_z], oz_ss.at[d - 1], oz_rs.at[from_z], s, from_z).wait_recv()
+    ox[x, y] = dot(p2[...], oz[...].reshape(NZ * OM, 128)).astype(BF)
+
+    def oy_copy(d):
+        to = lax.rem(y + d, NY)
+        return remote(ox.at[x, y], ox.at[x, y], oy_ss.at[d - 1], oy_rs.at[y], at(to, x), z)
+
+    for d in range(1, NY):
+        oy_copy(d).start()
+
     loads[6].wait()
     for h in range(H):
         low(0, h)
@@ -298,7 +359,49 @@
     )
     full_t = dot(tall, cols_of)
     c_l = idiv(imod(iota((CH * 2 * OWN, NC * MSG), 1), MSG), R)
+    w_third = jnp.sum(third * weight.astype(F32), axis=1, keepdims=True)
+    w_tall = dot(spread_t, jnp.broadcast_to(w_third, (2 * OWN, 128)).astype(BF))[:, :OM]
+    o_q, o_m = iota((CH * 2 * OWN, OM), 0), iota((CH * 2 * OWN, OM), 1)
+    o_ok = (idiv(o_m, 2) == idiv(o_q, 2 * OWN)) & (imod(o_m, 2) == imod(idiv(o_q, OWN), 2))
+    co[...] = jnp.where(o_ok, w_tall, 0.0).astype(BF)
     cm[...] = jnp.where(c_l == idiv(iota((CH * 2 * OWN, NC * MSG), 0), 2 * OWN), full_t, 0.0).astype(BF)
+
+    def ox_copy(d, from_y):
+        return remote(
+            ox.at[x, from_y], ox.at[x, from_y], ox_ss.at[d - 1, from_y], ox_rs.at[x, from_y],
+            at(y, lax.rem(x + d, NX)), z,
+        )
+
+    def ox_send():
+        @pl.loop(0, NY)
+        def _(dy):
+            from_y = lax.rem(y + dy, NY)
+
+            @pl.when(dy > 0)
+            def _():
+                remote(
+                    ox.at[x, from_y], ox.at[x, from_y], ox_ss.at[0, from_y], oy_rs.at[from_y], at(from_y, x), z
+                ).wait_recv()
+
+            for d in range(1, NX):
+                ox_copy(d, from_y).start()
+
+    def ox_take():
+        for d in range(NX):
+            from_x = lax.rem(x + d, NX)
+            if d:
+                @pl.loop(0, NY)
+                def _(from_y):
+                    remote(
+                        ox.at[from_x, from_y], ox.at[from_x, from_y], ox_ss.at[d - 1, from_y],
+                        ox_rs.at[from_x, from_y], at(y, from_x), z,
+                    ).wait_recv()
+            for c in range(CH):
+                width = min(128, HALF - 128 * c)
+                piece = ox[from_x, :, OWN * c:OWN * (c + 1), :].reshape(NR, 128)
+                slots[OV + d, :, 128 * c:128 * c + width] = piece[:, :width]
+            for h in range(H):
+                low(OV + d, h)
 
     for k in (1, 2, 3):
         for h in range(H):
@@ -312,10 +415,13 @@
                 ag_copy(far_from, FAR, h, far_to).start()
             low(k, h)
             low(k + 3, h)
+        if k == 1:
+            ox_send()
     loads[7].wait()
     for h in range(H):
         ag_copy(far_from, FAR, h, far_to).wait_recv()
         low(FAR, h)
+    ox_take()
 
     def expert(slot_at, h):
         lo_copy(slot_at, h).wait_recv()
@@ -341,6 +447,61 @@
         q_copy(3, 2, h, dn).start()
         qs[6, rows(h)] = (above + jnp.where(p == 0, 0.0, got)).astype(BF)
         q_copy(6, 5, h, up).start()
+
+    def or_copy(d):
+        return remote(
+            obuf.at[d], oret.at[x], or_ss.at[d - 1], or_rs.at[x], at(y, lax.rem(x + d, NX)), z
+        )
+
+    def oyr_copy(d):
+        to = lax.rem(y + d, NY)
+        return remote(osel.at[to], oyr.at[y], oyr_ss.at[d - 1], oyr_rs.at[y], at(to, x), z)
+
+    def ozr_copy(d):
+        to = lax.rem(z + d, NZ)
+        return remote(ozs.at[to], ozr.at[z], ozr_ss.at[d - 1], ozr_rs.at[z], s, to)
+
+    def ov_expert():
+        for d in (2, 1, 3, 0):
+            for h in range(H):
+                value = expert(OV + d, h).astype(BF)
+                n = SB // OWN
+                for c in range(CH):
+                    piece = value[:, 128 * c:128 * (c + 1)]
+                    if piece.shape[1] < 128:
+                        piece = jnp.concatenate([piece, jnp.zeros((SB, 128 * CH - HALF), BF)], axis=1)
+                    obuf[d, n * h:n * (h + 1), OWN * c:OWN * (c + 1), :] = piece.reshape(n, OWN, 128)
+            if d:
+                or_copy(d).start()
+
+    def ov_back_y():
+        for d in range(1, NX):
+            from_x = lax.rem(x + d, NX)
+            remote(obuf.at[d], oret.at[from_x], or_ss.at[d - 1], or_rs.at[from_x], at(y, from_x), z).wait_recv()
+
+        @pl.loop(0, NY)
+        def _(to_y):
+            acc = jnp.where(hot_x == x.astype(F32), obuf[0, to_y].astype(F32), 0.0)
+            for d in range(1, NX):
+                from_x = lax.rem(x + d, NX)
+                acc = jnp.where(hot_x == from_x.astype(F32), oret[from_x, to_y].astype(F32), acc)
+            osel[to_y] = acc.astype(BF)
+
+        for d in range(1, NY):
+            oyr_copy(d).start()
+
+    def ov_back_z():
+        acc = jnp.where(hot_y == y.astype(F32), osel[y].astype(F32), 0.0)
+        for d in range(1, NY):
+            from_y = lax.rem(y + d, NY)
+            remote(osel.at[from_y], oyr.at[from_y], oyr_ss.at[d - 1], oyr_rs.at[from_y], at(from_y, x), z).wait_recv()
+            acc = jnp.where(hot_y == from_y.astype(F32), oyr[from_y].astype(F32), acc)
+        ozs[...] = dot(p2t[...], acc.astype(BF)).astype(BF).reshape(NZ, OM, 128)
+        for d in range(1, NZ):
+            ozr_copy(d).start()
+        ozr[z] = ozs[z]
+
+    ov_expert()
     for k in (2, 1):
         for h in range(H):
             below, above = expert(k, h), expert(k + 3, h)
@@ -350,6 +511,8 @@
             q_copy(k + 3, k + 3, h, up).wait_recv()
             qs[k + 3, rows(h)] = (above + racc[k + 3, rows(h)].astype(F32)).astype(BF)
             q_copy(k + 3, k + 2, h, up).start()
+        if k == 2:
+            ov_back_y()
 
     def a2_copy(to):
         return remote(sb2.at[to], rb2.at[chip], a2_ss.at[to], a2_rs.at[chip], to * 2 + p, z)
@@ -376,7 +539,12 @@
                 def _():
                     a2_copy(to).start()
 
+    ov_back_z()
     rb2[chip] = sb2[chip]
+    for d in range(1, NZ):
+        from_z = lax.rem(z + d, NZ)
+        remote(ozs.at[from_z], ozr.at[from_z], ozr_ss.at[d - 1], ozr_rs.at[from_z], s, from_z).wait_recv()
+    third_sum = jnp.sum(ozr[...].astype(F32), axis=0).astype(BF)
 
     @pl.loop(0, NC)
     def _(src):
@@ -384,7 +552,8 @@
         def _():
             remote(sb2.at[src], rb2.at[src], a2_ss.at[src], a2_rs.at[src], src * 2 + p, z).wait_recv()
 
-    out = dot(cm[...], rb2[...].reshape(NC * MSG, 128)).astype(BF).reshape(CH, 2 * OWN, 128)
+    out = dot(cm[...], rb2[...].reshape(NC * MSG, 128)) + dot(co[...], third_sum)
+    out = out.astype(BF).reshape(CH, 2 * OWN, 128)
     cm_out = xbuf
     cm_out[...] = out
     theirs = pl.ds(pl.multiple_of((1 - p) * OWN, OWN), OWN)
@@ -403,51 +572,66 @@
     f_copy.wait_send()
     for d in range(1, NZ):
         rs_copy(d).wait_send()
+        oz_copy(d).wait_send()
+        oy_copy(d).wait_send()
+        oyr_copy(d).wait_send()
+        ozr_copy(d).wait_send()
+    for d in range(1, NX):
+        or_copy(d).wait_send()
+
+        @pl.loop(0, NY)
+        def _(from_y):
+            ox_copy(d, from_y).wait_send()
 
     @pl.loop(1, NC)
     def _(d):
         a1_copy(d).wait_send()
         a2_copy(lax.rem(chip + d, NC)).wait_send()
 
-    for slot_at in range(8):
+    for slot_at in range(OV + NX):
         for h in range(H):
             lo_copy(slot_at, h).wait_send()
-            if slot_at:
+            if 0 < slot_at < OV:
                 ag_copy(0, slot_at, h, up).wait_send()
                 q_copy(slot_at, slot_at, h, up).wait_send()
 
 
 def per_device(q, kv, wo, res, gain, ids, weights, w_in, w_out):
-    info = jnp.concatenate([ids.astype(F32), weights.astype(F32), jnp.zeros((TOK, 128 - 2 * TOP), F32)], axis=1)
     vm = pltpu.VMEM
     dma = pltpu.SemaphoreType.DMA
     scratch = [
-        vm((TOK, 512), BF), vm((2, TOK, 128), BF), vm((512, D), BF), vm((OWN, D), BF), vm((1, D), F32),
-        vm((2, OWN, 128), F32), vm((HALF, 384), BF), vm((192, HALF), BF),
+        vm((TOK, 512), BF), vm((2, TOK, 128), BF), vm((D, 512), BF), vm((OWN, D), BF), vm((D,), F32),
+        vm((TOP, TOK), I32), vm((TOP, TOK), BF), vm((2 * TOP, TOK), F32), vm((2, OWN, 128), F32), vm((HALF, 384), BF), vm((192, HALF), BF),
         vm((TOK, 512), BF), vm((NZ, OWN, D), F32), vm((NZ, OWN, D), BF), vm((NZ - 1, OWN, D), BF),
         vm((2, CH, OWN, 128), BF), vm((CH, 2 * OWN, 128), BF),
         vm((NC * MSG, CH * 2 * OWN), BF), vm((CH * 2 * OWN, NC * MSG), BF),
         vm((CH * GR, GS * MSG), BF), vm((GS * MSG, CH * GR), BF),
         vm((NC, MSG, 128), BF), vm((NC, MSG, 128), BF),
-        vm((8, NR, HALF), BF), vm((8, NR, 384), BF), vm((8, NR, 384), BF),
+        vm((OV + NX, NR, HALF), BF), vm((OV + NX, NR, 384), BF), vm((OV + NX, NR, 384), BF),
         vm((8, NR, HALF), BF), vm((8, NR, HALF), BF),
         vm((NC, MSG, 128), BF), vm((NC, MSG, 128), BF),
         vm((2, CH, OWN, 128), BF), vm((CH, OWN, 128), BF),
-        dma((8,)), dma, dma, dma, dma, dma((NZ - 1,)), dma((NZ - 1,)), dma, dma,
-        dma((NC,)), dma((NC,)), dma((8, H)), dma((8, H)), dma((8, H)), dma((8, H)),
+        vm((OM, CH * 2 * OWN), BF), vm((CH * 2 * OWN, OM), BF), vm((OB, NZ * OM), BF), vm((NZ * OM, OB), BF),
+        vm((OM, 128), BF), vm((NZ, OM, 128), BF), vm((NX, NY, OB, 128), BF), vm((NX, NY, OB, 128), BF),
+        vm((NX, NY, OB, 128), BF), vm((NY, OB, 128), BF), vm((NY, OB, 128), BF),
+        vm((NZ, OM, 128), BF), vm((NZ, OM, 128), BF),
+        dma((9,)), dma, dma, dma, dma, dma((NZ - 1,)), dma((NZ - 1,)), dma, dma,
+        dma((NC,)), dma((NC,)), dma((8, H)), dma((8, H)), dma((OV + NX, H)), dma((OV + NX, H)),
         dma((8, H)), dma((8, H)), dma((NC,)), dma((NC,)), dma, dma,
+        dma((NZ,)), dma((NZ,)), dma((NY,)), dma((NY,)), dma((NX, NY)), dma((NX, NY)), dma((NX,)), dma((NX,)),
+        dma((NY,)), dma((NY,)), dma((NZ,)), dma((NZ,)),
     ]
     return pl.pallas_call(
         kernel,
         out_shape=(jax.ShapeDtypeStruct((OWN, D), BF), jax.ShapeDtypeStruct((OWN, D), BF)),
-        in_specs=[pl.BlockSpec(memory_space=pl.ANY)] * 8,
+        in_specs=[pl.BlockSpec(memory_space=pl.ANY)] * 9,
         out_specs=(pl.BlockSpec(memory_space=vm), pl.BlockSpec(memory_space=vm)),
         scratch_shapes=scratch,
         compiler_params=pltpu.CompilerParams(
             collective_id=0, has_side_effects=True, vmem_limit_bytes=58 * 1024 * 1024
         ),
         cost_estimate=pl.CostEstimate(flops=4_000_000_000, bytes_accessed=8_000_000, transcendentals=300_000),
-    )(q, kv.reshape(TOK, 128), wo, res, gain.reshape(1, D), info, w_in, w_out)
+    )(q, kv.reshape(TOK, 128), wo.T, res, gain, ids.T, weights.T, w_in, w_out)
 
 
 def solution(mesh):

time: 185 us -> 148 us (0.80)
  the two profiles are of different devices: /device:TPU:57 before, /device:TPU:1 now
where the time goes in v2:
time: 148 us; the launch traced here: 146 us
  Pallas kernels  142 us (96%)
  local copies, waits for them, and re-layouts  3.07 us (2%)
    pallas_call x1, Pallas kernels, per_device(): pl.pallas_call(kernel, out_shape=(jax.ShapeDtypeStruct((OWN, D), BF), jax...  142 us
    unnamed x2, local copies, waits for them, and re-layouts  3.07 us

profile of v2, /device:TPU:1, one launch (start us, length us, event | category | flops | bytes accessed | tf_op | source)
XLA Modules:
  0.0 145.5 jit_solution(11709629416229907950)
XLA Ops:
  0.6 141.8 %shard_map.104 = (bf16[16,2880]{1,0:T(8,128)(2,1)}, bf16[16,2880]{1,0:T(8,128)(2,1)}) custom-call(bf16[128,512]{1,0:T(8,128)(2,1)} %q_hbm.1, bf16[128,128]{1,0:T(8,128)(2,1)} %bitcast.5, bf16[2880,512]{1,0:T(8,128)(2,1)} %bitcast.4, bf16[16,2880]{1,0:T(8,128)(2,1)} %res_hbm.1, f32[2880]{0:T(1024)} %gain_hbm.1, s32[4,128]{1,0:T(4,128)} %bitcast.6, ...), custom_call_target="tpu_custom_call" | custom-call | flops 4000000000 | bytes 8000000 | tf_op jit(solution)/shard_map/pallas_call | solution.py:624
  142.5 1.5 %copy.13 = bf16[16,2880]{1,0:T(8,128)(2,1)} copy(bf16[16,2880]{1,0:T(8,128)(2,1)} %get-tuple-element.4) | data formatting | bytes 184320
  144.0 1.5 %copy.14 = bf16[16,2880]{1,0:T(8,128)(2,1)} copy(bf16[16,2880]{1,0:T(8,128)(2,1)} %get-tuple-element.5) | data formatting | bytes 184320

commit v3 on v2

--- a/solution.py
+++ b/solution.py
@@ -26,7 +26,13 @@
 FAR = 7
 OV = 8
 OM = 32
+PIECES = ((0, 1536), (1536, D))
 OB = CH * OWN
+
+NEAR = sorted(
+    [(dy, dx) for dy in range(-3, 5) for dx in range(-1, 3)], key=lambda o: (abs(o[0]) + abs(o[1]), o)
+)
+SEEN = [NEAR.index(((3 - dy) % NY - 3, (1 - dx) % NX - 1)) for dy, dx in NEAR]
 
 
 def idiv(v, n):
@@ -61,7 +67,7 @@
     q_v, kv2, wo_v, res_v, gain_v, ids_v, rw_v, both, info2, win_v, wout_v,
     att_v, own_f, ps, rs, stage, xbuf, dm, cm, pm, pt,
     sb1, rb1, slots, low_own, low_oth, qs, racc, sb2, rb2, fin, fsend,
-    om, co, p2, p2t, osend, oz, ox, obuf, oret, osel, oyr, ozs, ozr,
+    om, co, p2, p2t, osend, oz, ox, obuf, ofar, oret, osel, oyr, ozs, ozr,
     load_sem, kv_ss, kv_rs, info_ss, info_rs, rs_ss, rs_rs, st_ss, st_rs,
     a1_ss, a1_rs, ag_ss, ag_rs, lo_ss, lo_rs, q_ss, q_rs, a2_ss, a2_rs, f_ss, f_rs,
     oz_ss, oz_rs, oy_ss, oy_rs, ox_ss, ox_rs, or_ss, or_rs, oyr_ss, oyr_rs, ozr_ss, ozr_rs,
@@ -132,6 +138,30 @@
     info2[p, :, 0:2 * TOP] = dot_nt(chosen, both[...].astype(BF))
     info_copy = remote(info2.at[p], info2.at[p], info_ss, info_rs, other, z)
     info_copy.start()
+    def perm2(shape, a_dim):
+        i, j = iota(shape, a_dim), iota(shape, 1 - a_dim)
+        inner = imod(j, OM)
+        return ones(
+            (idiv(i, OWN) == idiv(inner, 2))
+            & (idiv(imod(i, OWN), 2) == idiv(j, OM))
+            & (imod(i, 2) == imod(inner, 2))
+        )
+
+    p2[...] = perm2((OB, NZ * OM), 0)
+    p2t[...] = perm2((NZ * OM, OB), 1)
+
+    def perm(shape, a_dim):
+        i, j = iota(shape, a_dim), iota(shape, 1 - a_dim)
+        inner = imod(j, MSG)
+        return ones(
+            (idiv(i, GR) == idiv(inner, R))
+            & (idiv(imod(i, GR), R) == idiv(j, MSG))
+            & (imod(i, R) == imod(inner, R))
+            & (inner < CH * R)
+        )
+
+    pm[...] = perm((CH * GR, GS * MSG), 0)
+    pt[...] = perm((GS * MSG, CH * GR), 1)
     loads[1].wait()
     kv_copy.wait_recv()
 
@@ -156,19 +186,36 @@
             acc = part if acc is None else acc + part
         att_v[:, 128 * pair:128 * (pair + 1)] = acc.astype(BF)
 
+    far_from = 3 + 3 * p
+    far_to = lax.rem(z + 1 + (NZ - 2) * p, NZ)
+    far_back = lax.rem(z + NZ - 1 + 2 * p, NZ)
+
+    def h_copy(slot_at, dst, c, head):
+        lo, hi = PIECES[c]
+        return remote(
+            ps.at[slot_at, :, lo:hi], rs.at[dst, :, lo:hi], rs_ss.at[slot_at, c], rs_rs.at[dst, c], s, head
+        )
+
+    def block(d, c):
+        lo, hi = PIECES[c]
+        return own_f[lax.rem(z + d + NZ, NZ), :, lo:hi]
+
+    def got_h(dst, c):
+        lo, hi = PIECES[c]
+        h_copy(FAR, dst, c, up).wait_recv()
+        return rs[dst, :, lo:hi].astype(F32)
+
+    def send_h(slot_at, dst, c, head, value):
+        lo, hi = PIECES[c]
+        ps[slot_at, :, lo:hi] = value.astype(BF)
+        h_copy(slot_at, dst, c, head).start()
+
     loads[3].wait()
-    for n0 in range(0, D, 512):
-        n1 = min(D, n0 + 512)
-        part = dot_nt(att_v[...], wo_v[n0:n1]).reshape(NZ, OWN, n1 - n0)
-        own_f[:, :, n0:n1] = part
-        ps[:, :, n0:n1] = part.astype(BF)
-
-    def rs_copy(d):
-        to = lax.rem(z + d, NZ)
-        return remote(ps.at[to], rs.at[d - 1], rs_ss.at[d - 1], rs_rs.at[d - 1], s, to)
-
-    for d in (4, 3, 5, 2, 6, 1, 7):
-        rs_copy(d).start()
+    for c, (lo, hi) in enumerate(PIECES):
+        for n0 in range(lo, hi, 512):
+            n1 = min(hi, n0 + 512)
+            own_f[:, :, n0:n1] = dot_nt(att_v[...], wo_v[n0:n1]).reshape(NZ, OWN, n1 - n0)
+        send_h(FAR, FAR, c, far_back, block(4, c))
 
     info_copy.wait_recv()
     inf = info2[...].reshape(2 * OWN, 128)
@@ -185,6 +232,12 @@
     slot = dot(before, named).astype(BF)
     ra = iota((NC * R, 128), 0)
     expand = ones(idiv(ra, R) == iota((NC * R, 128), 1))
+
+    for c in range(2):
+        got = got_h(FAR, c)
+        send_h(3, 2, c, dn, block(-3, c) + jnp.where(p == 0, got, 0.0))
+        send_h(6, 5, c, up, block(3, c) + jnp.where(p == 0, 0.0, got))
+
     r_i = imod(iota((NC * R, 2 * OWN), 0), R)
     t_i = iota((NC * R, 2 * OWN), 1)
     want = r_i - idiv(r_i, CAP) * CAP
@@ -205,6 +258,11 @@
     full = dot(rows_of, wide).reshape(NC, MSG, CH * 2 * OWN) * chunk_ok[None]
     dm[...] = full.reshape(NC * MSG, CH * 2 * OWN).astype(BF)
 
+
+    for c in range(2):
+        send_h(2, 1, c, dn, block(-2, c) + got_h(2, c))
+        send_h(5, 4, c, up, block(2, c) + got_h(5, c))
+
     third = jnp.where((named > 0.5) & (slot > 1.5), 1.0, 0.0)
     third_row = dot_nt(jnp.ones((8, 128), BF), third.astype(BF))[0:1]
     third_wide = dot(jnp.broadcast_to(third_row, (8, 2 * OWN)).astype(BF), spread)[0:1]
@@ -216,37 +274,15 @@
     hot_x = jnp.sum(hot * imod(e_row, NX).astype(F32), axis=1, keepdims=True)
     hot_y = jnp.sum(hot * idiv(e_row, NX).astype(F32), axis=1, keepdims=True)
 
-    def perm2(shape, a_dim):
-        i, j = iota(shape, a_dim), iota(shape, 1 - a_dim)
-        inner = imod(j, OM)
-        return ones(
-            (idiv(i, OWN) == idiv(inner, 2))
-            & (idiv(imod(i, OWN), 2) == idiv(j, OM))
-            & (imod(i, 2) == imod(inner, 2))
-        )
-
-    p2[...] = perm2((OB, NZ * OM), 0)
-    p2t[...] = perm2((NZ * OM, OB), 1)
-
-    def perm(shape, a_dim):
-        i, j = iota(shape, a_dim), iota(shape, 1 - a_dim)
-        inner = imod(j, MSG)
-        return ones(
-            (idiv(i, GR) == idiv(inner, R))
-            & (idiv(imod(i, GR), R) == idiv(j, MSG))
-            & (imod(i, R) == imod(inner, R))
-            & (inner < CH * R)
-        )
-
-    pm[...] = perm((CH * GR, GS * MSG), 0)
-    pt[...] = perm((GS * MSG, CH * GR), 1)
+
+    for c in range(2):
+        send_h(1, 0, c, dn, block(-1, c) + got_h(1, c))
+        send_h(4, 3, c, up, block(1, c) + got_h(4, c))
 
     loads[4].wait()
     loads[5].wait()
-    total = res_v[...].astype(F32) + own_f[z]
-    for d in (1, 7, 2, 6, 3, 5, 4):
-        rs_copy(d).wait_recv()
-        total = total + rs[d - 1].astype(F32)
+    total = jnp.concatenate([block(0, c) + (got_h(0, c) + got_h(3, c)) for c in range(2)], axis=1)
+    total = total + res_v[...].astype(F32)
     stream_ref[...] = total.astype(BF)
     mean_square = jnp.mean(total * total, axis=-1, keepdims=True)
     normed = (total * lax.rsqrt(mean_square + 1e-5) * gain_v[...].reshape(1, D)).astype(BF)
@@ -279,69 +315,17 @@
     msgs = dot(dm[...], xbuf[...].reshape(CH * 2 * OWN, 128)).astype(BF)
     sb1[...] = msgs.reshape(NC, MSG, 128)
 
-    def a1_copy(d):
-        to = lax.rem(chip + d, NC)
-        return remote(sb1.at[to], rb1.at[chip], a1_ss.at[to], a1_rs.at[chip], to * 2 + p, z)
-
-    @pl.loop(1, NC)
-    def _(d):
-        a1_copy(d).start()
-
-    rb1[chip] = sb1[chip]
-
-    def a1_wait(src):
-        @pl.when(src != chip)
-        def _():
-            remote(sb1.at[src], rb1.at[src], a1_ss.at[src], a1_rs.at[src], src * 2 + p, z).wait_recv()
-
-    far_from = 3 + 3 * p
-    far_to = lax.rem(z + 1 + (NZ - 2) * p, NZ)
-    far_back = lax.rem(z + NZ - 1 + 2 * p, NZ)
-
-    def rows(h):
-        return pl.ds(h * SB, SB)
-
-    def ag_copy(src, dst, h, head):
-        return remote(
-            slots.at[src, rows(h)], slots.at[dst, rows(h)],
-            ag_ss.at[dst, h], ag_rs.at[dst, h], s, head,
-        )
-
-    def lo_copy(slot_at, h):
-        return remote(
-            low_own.at[slot_at, rows(h)], low_oth.at[slot_at, rows(h)],
-            lo_ss.at[slot_at, h], lo_rs.at[slot_at, h], other, z,
-        )
-
-    def low(slot_at, h):
-        low_own[slot_at, rows(h)] = dot(slots[slot_at, rows(h)], win_v[...]).astype(BF)
-        lo_copy(slot_at, h).start()
-
-    for h in range(H):
-        for g in range(h * GH, (h + 1) * GH):
-            for i in range(GS):
-                a1_wait(g * GS + i)
-            got = dot(pm[...], rb1[GS * g:GS * (g + 1)].reshape(GS * MSG, 128)).astype(BF)
-            for c in range(CH):
-                width = min(128, HALF - 128 * c)
-                slots[0, GR * g:GR * (g + 1), 128 * c:128 * c + width] = got[GR * c:GR * (c + 1), :width]
-        ag_copy(0, 1, h, up).start()
-        ag_copy(0, 4, h, dn).start()
-    for d in range(1, NZ):
-        from_z = lax.rem(z + d, NZ)
-        remote(osend, oz.at[from_z], oz_ss.at[d - 1], oz_rs.at[from_z], s, from_z).wait_recv()
-    ox[x, y] = dot(p2[...], oz[...].reshape(NZ * OM, 128)).astype(BF)
-
-    def oy_copy(d):
-        to = lax.rem(y + d, NY)
-        return remote(ox.at[x, y], ox.at[x, y], oy_ss.at[d - 1], oy_rs.at[y], at(to, x), z)
-
-    for d in range(1, NY):
-        oy_copy(d).start()
-
-    loads[6].wait()
-    for h in range(H):
-        low(0, h)
+    def near(r):
+        dy, dx = NEAR[r]
+        return lax.rem(y + dy + NY, NY) * NX + lax.rem(x + dx + NX, NX)
+
+    def a1_copy(r):
+        to = near(r)
+        return remote(sb1.at[to], rb1.at[SEEN[r]], a1_ss.at[r], a1_rs.at[SEEN[r]], to * 2 + p, z)
+
+    for r in range(1, NC):
+        a1_copy(r).start()
+    rb1[0] = sb1[chip]
 
     e_l = iota((2 * OWN, NC * R), 1)
     r_l = imod(e_l, R)
@@ -366,43 +350,97 @@
     co[...] = jnp.where(o_ok, w_tall, 0.0).astype(BF)
     cm[...] = jnp.where(c_l == idiv(iota((CH * 2 * OWN, NC * MSG), 0), 2 * OWN), full_t, 0.0).astype(BF)
 
-    def ox_copy(d, from_y):
+    def a1_wait(r):
+        if r:
+            a1_copy(SEEN[r]).wait_recv()
+
+    def rows(h):
+        return pl.ds(h * SB, SB)
+
+    def ag_copy(src, dst, h, head):
         return remote(
-            ox.at[x, from_y], ox.at[x, from_y], ox_ss.at[d - 1, from_y], ox_rs.at[x, from_y],
-            at(y, lax.rem(x + d, NX)), z,
-        )
-
-    def ox_send():
-        @pl.loop(0, NY)
-        def _(dy):
-            from_y = lax.rem(y + dy, NY)
-
-            @pl.when(dy > 0)
-            def _():
-                remote(
-                    ox.at[x, from_y], ox.at[x, from_y], ox_ss.at[0, from_y], oy_rs.at[from_y], at(from_y, x), z
-                ).wait_recv()
-
-            for d in range(1, NX):
-                ox_copy(d, from_y).start()
-
-    def ox_take():
-        for d in range(NX):
-            from_x = lax.rem(x + d, NX)
-            if d:
-                @pl.loop(0, NY)
-                def _(from_y):
-                    remote(
-                        ox.at[from_x, from_y], ox.at[from_x, from_y], ox_ss.at[d - 1, from_y],
-                        ox_rs.at[from_x, from_y], at(y, from_x), z,
-                    ).wait_recv()
+            slots.at[src, rows(h)], slots.at[dst, rows(h)],
+            ag_ss.at[dst, h], ag_rs.at[dst, h], s, head,
+        )
+
+    def lo_copy(slot_at, h):
+        return remote(
+            low_own.at[slot_at, rows(h)], low_oth.at[slot_at, rows(h)],
+            lo_ss.at[slot_at, h], lo_rs.at[slot_at, h], other, z,
+        )
+
+    def low(slot_at, h):
+        low_own[slot_at, rows(h)] = dot(slots[slot_at, rows(h)], win_v[...]).astype(BF)
+        lo_copy(slot_at, h).start()
+
+    for h in range(H):
+        for g in range(h * GH, (h + 1) * GH):
+            for i in range(GS):
+                a1_wait(g * GS + i)
+            got = dot(pm[...], rb1[GS * g:GS * (g + 1)].reshape(GS * MSG, 128)).astype(BF)
             for c in range(CH):
                 width = min(128, HALF - 128 * c)
-                piece = ox[from_x, :, OWN * c:OWN * (c + 1), :].reshape(NR, 128)
-                slots[OV + d, :, 128 * c:128 * c + width] = piece[:, :width]
-            for h in range(H):
-                low(OV + d, h)
-
+                slots[0, GR * g:GR * (g + 1), 128 * c:128 * c + width] = got[GR * c:GR * (c + 1), :width]
+        ag_copy(0, 1, h, up).start()
+        ag_copy(0, 4, h, dn).start()
+    for d in range(1, NZ):
+        from_z = lax.rem(z + d, NZ)
+        remote(osend, oz.at[from_z], oz_ss.at[d - 1], oz_rs.at[from_z], s, from_z).wait_recv()
+    ox[x, y] = dot(p2[...], oz[...].reshape(NZ * OM, 128)).astype(BF)
+
+    def oy_copy(d):
+        to = lax.rem(y + d, NY)
+        return remote(ox.at[x, y], ox.at[x, y], oy_ss.at[d - 1], oy_rs.at[y], at(to, x), z)
+
+    for d in range(1, NY):
+        oy_copy(d).start()
+
+    loads[6].wait()
+    for h in range(H):
+        low(0, h)
+
+    right, left = lax.rem(x + 1, NX), lax.rem(x + NX - 1, NX)
+
+    def ox_copy(way, from_x, from_y):
+        return remote(
+            ox.at[from_x, from_y], ox.at[from_x, from_y], ox_ss.at[way, from_y], ox_rs.at[from_x, from_y],
+            at(y, right if way in (0, 2) else left), z,
+        )
+
+    def ox_send(dy):
+        from_y = lax.rem(y + dy, NY)
+        if dy:
+            remote(
+                ox.at[x, from_y], ox.at[x, from_y], ox_ss.at[0, from_y], oy_rs.at[from_y], at(from_y, x), z
+            ).wait_recv()
+        ox_copy(0, x, from_y).start()
+        ox_copy(1, x, from_y).start()
+
+    def ox_take(d):
+        from_x = lax.rem(x + d, NX)
+        if d:
+            for from_y in range(NY):
+                ox_copy(0, from_x, from_y).wait_recv()
+                if d == 3 and from_y < 4:
+                    ox_copy(2, left, from_y).start()
+                if d == 1 and from_y >= 4:
+                    ox_copy(3, right, from_y).start()
+        for c in range(CH):
+            width = min(128, HALF - 128 * c)
+            piece = ox[from_x, :, OWN * c:OWN * (c + 1), :].reshape(NR, 128)
+            slots[OV + d, :, 128 * c:128 * c + width] = piece[:, :width]
+        for h in range(H):
+            low(OV + d, h)
+
+    ox_send(0)
+    aside = {
+        (1, 0): (lambda: (ox_send(1), ox_send(7))),
+        (1, 1): (lambda: (ox_send(2), ox_send(6))),
+        (2, 0): (lambda: (ox_send(3), ox_send(5), ox_send(4))),
+        (2, 1): (lambda: ox_take(0)),
+        (3, 0): (lambda: ox_take(3)),
+        (3, 1): (lambda: ox_take(1)),
+    }
     for k in (1, 2, 3):
         for h in range(H):
             ag_copy(0, k, h, up).wait_recv()
@@ -415,13 +453,11 @@
                 ag_copy(far_from, FAR, h, far_to).start()
             low(k, h)
             low(k + 3, h)
-        if k == 1:
-            ox_send()
+            aside[k, h]()
     loads[7].wait()
     for h in range(H):
         ag_copy(far_from, FAR, h, far_to).wait_recv()
         low(FAR, h)
-    ox_take()
 
     def expert(slot_at, h):
         lo_copy(slot_at, h).wait_recv()
@@ -439,6 +475,7 @@
     for h in range(H):
         qs[FAR, rows(h)] = expert(FAR, h).astype(BF)
         q_copy(FAR, FAR, h, far_back).start()
+    ox_take(2)
     for h in range(H):
         below, above = expert(3, h), expert(6, h)
         q_copy(FAR, FAR, h, far_back).wait_recv()
@@ -448,9 +485,16 @@
         qs[6, rows(h)] = (above + jnp.where(p == 0, 0.0, got)).astype(BF)
         q_copy(6, 5, h, up).start()
 
-    def or_copy(d):
+    def of_copy(way):
+        part = slice(0, 4) if way == 0 else slice(4, 8)
         return remote(
-            obuf.at[d], oret.at[x], or_ss.at[d - 1], or_rs.at[x], at(y, lax.rem(x + d, NX)), z
+            obuf.at[2, part], ofar.at[part], or_ss.at[way], or_rs.at[way], at(y, left if way == 0 else right), z
+        )
+
+    def or_copy(way):
+        return remote(
+            obuf.at[3 - 2 * way], oret.at[way], or_ss.at[2 + way], or_rs.at[2 + way],
+            at(y, left if way == 0 else right), z,
         )
 
     def oyr_copy(d):
@@ -461,32 +505,43 @@
         to = lax.rem(z + d, NZ)
         return remote(ozs.at[to], ozr.at[z], ozr_ss.at[d - 1], ozr_rs.at[z], s, to)
 
-    def ov_expert():
-        for d in (2, 1, 3, 0):
-            for h in range(H):
-                value = expert(OV + d, h).astype(BF)
-                n = SB // OWN
-                for c in range(CH):
-                    piece = value[:, 128 * c:128 * (c + 1)]
-                    if piece.shape[1] < 128:
-                        piece = jnp.concatenate([piece, jnp.zeros((SB, 128 * CH - HALF), BF)], axis=1)
-                    obuf[d, n * h:n * (h + 1), OWN * c:OWN * (c + 1), :] = piece.reshape(n, OWN, 128)
-            if d:
-                or_copy(d).start()
+    here = hot_x == x.astype(F32)
+
+    def ov_expert(d):
+        for h in range(H):
+            value = expert(OV + d, h).astype(BF)
+            n = SB // OWN
+            for c in range(CH):
+                piece = value[:, 128 * c:128 * (c + 1)]
+                if piece.shape[1] < 128:
+                    piece = jnp.concatenate([piece, jnp.zeros((SB, 128 * CH - HALF), BF)], axis=1)
+                obuf[d, n * h:n * (h + 1), OWN * c:OWN * (c + 1), :] = piece.reshape(n, OWN, 128)
+
+    def ov_far():
+        ov_expert(2)
+        for way in range(2):
+            of_copy(way).start()
+
+    def ov_near():
+        for way in range(2):
+            ov_expert(3 - 2 * way)
+        for way in range(2):
+            of_copy(way).wait_recv()
+            for to_y in range(4 * way, 4 * way + 4):
+                mixed = jnp.where(here, obuf[3 - 2 * way, to_y].astype(F32), ofar[to_y].astype(F32))
+                obuf[3 - 2 * way, to_y] = mixed.astype(BF)
+            or_copy(way).start()
+        ov_expert(0)
 
     def ov_back_y():
-        for d in range(1, NX):
-            from_x = lax.rem(x + d, NX)
-            remote(obuf.at[d], oret.at[from_x], or_ss.at[d - 1], or_rs.at[from_x], at(y, from_x), z).wait_recv()
-
-        @pl.loop(0, NY)
-        def _(to_y):
-            acc = jnp.where(hot_x == x.astype(F32), obuf[0, to_y].astype(F32), 0.0)
-            for d in range(1, NX):
-                from_x = lax.rem(x + d, NX)
-                acc = jnp.where(hot_x == from_x.astype(F32), oret[from_x, to_y].astype(F32), acc)
-            osel[to_y] = acc.astype(BF)
-
+        for way in range(2):
+            or_copy(way).wait_recv()
+        for to_y in range(NY):
+            pass_by = 0 if to_y < 4 else 1
+            acc = oret[pass_by, to_y].astype(F32)
+            neighbour = left if to_y < 4 else right
+            acc = jnp.where(hot_x == neighbour.astype(F32), oret[1 - pass_by, to_y].astype(F32), acc)
+            osel[to_y] = jnp.where(here, obuf[0, to_y].astype(F32), acc).astype(BF)
         for d in range(1, NY):
             oyr_copy(d).start()
 
@@ -501,7 +556,7 @@
             ozr_copy(d).start()
         ozr[z] = ozs[z]
 
-    ov_expert()
+    ov_far()
     for k in (2, 1):
         for h in range(H):
             below, above = expert(k, h), expert(k + 3, h)
@@ -512,10 +567,13 @@
             qs[k + 3, rows(h)] = (above + racc[k + 3, rows(h)].astype(F32)).astype(BF)
             q_copy(k + 3, k + 2, h, up).start()
         if k == 2:
+            ov_near()
+        else:
             ov_back_y()
 
-    def a2_copy(to):
-        return remote(sb2.at[to], rb2.at[chip], a2_ss.at[to], a2_rs.at[chip], to * 2 + p, z)
+    def a2_copy(r):
+        to = near(r)
+        return remote(sb2.at[r], rb2.at[chip], a2_ss.at[r], a2_rs.at[chip], to * 2 + p, z)
 
     for h in range(H):
         value = expert(0, h)
@@ -530,17 +588,12 @@
             pieces.append(jnp.concatenate([last, jnp.zeros((GR, 128 * CH - HALF), BF)], axis=1))
             out = dot(pt[...], jnp.concatenate(pieces, axis=0)).astype(BF)
             sb2[GS * g:GS * (g + 1)] = out.reshape(GS, MSG, 128)
-
-            @pl.loop(0, GS)
-            def _(j):
-                to = g * GS + j
-
-                @pl.when(to != chip)
-                def _():
-                    a2_copy(to).start()
+            for r in range(GS * g, GS * (g + 1)):
+                if r:
+                    a2_copy(r).start()
 
     ov_back_z()
-    rb2[chip] = sb2[chip]
+    rb2[chip] = sb2[0]
     for d in range(1, NZ):
         from_z = lax.rem(z + d, NZ)
         remote(ozs.at[from_z], ozr.at[from_z], ozr_ss.at[d - 1], ozr_rs.at[from_z], s, from_z).wait_recv()
@@ -550,7 +603,7 @@
     def _(src):
         @pl.when(src != chip)
         def _():
-            remote(sb2.at[src], rb2.at[src], a2_ss.at[src], a2_rs.at[src], src * 2 + p, z).wait_recv()
+            remote(sb2.at[src], rb2.at[src], a2_ss.at[0], a2_rs.at[src], src * 2 + p, z).wait_recv()
 
     out = dot(cm[...], rb2[...].reshape(NC * MSG, 128)) + dot(co[...], third_sum)
     out = out.astype(BF).reshape(CH, 2 * OWN, 128)
@@ -571,22 +624,22 @@
     st_copy.wait_send()
     f_copy.wait_send()
     for d in range(1, NZ):
-        rs_copy(d).wait_send()
         oz_copy(d).wait_send()
         oy_copy(d).wait_send()
         oyr_copy(d).wait_send()
         ozr_copy(d).wait_send()
-    for d in range(1, NX):
-        or_copy(d).wait_send()
-
-        @pl.loop(0, NY)
-        def _(from_y):
-            ox_copy(d, from_y).wait_send()
-
-    @pl.loop(1, NC)
-    def _(d):
-        a1_copy(d).wait_send()
-        a2_copy(lax.rem(chip + d, NC)).wait_send()
+        for c in range(2):
+            h_copy(d, d, c, up).wait_send()
+    for way in range(2):
+        of_copy(way).wait_send()
+        or_copy(way).wait_send()
+    for from_y in range(NY):
+        ox_copy(0, x, from_y).wait_send()
+        ox_copy(1, x, from_y).wait_send()
+        ox_copy(2 if from_y < 4 else 3, x, from_y).wait_send()
+    for r in range(1, NC):
+        a1_copy(r).wait_send()
+        a2_copy(r).wait_send()
 
     for slot_at in range(OV + NX):
         for h in range(H):
@@ -602,7 +655,7 @@
     scratch = [
         vm((TOK, 512), BF), vm((2, TOK, 128), BF), vm((D, 512), BF), vm((OWN, D), BF), vm((D,), F32),
         vm((TOP, TOK), I32), vm((TOP, TOK), BF), vm((2 * TOP, TOK), F32), vm((2, OWN, 128), F32), vm((HALF, 384), BF), vm((192, HALF), BF),
-        vm((TOK, 512), BF), vm((NZ, OWN, D), F32), vm((NZ, OWN, D), BF), vm((NZ - 1, OWN, D), BF),
+        vm((TOK, 512), BF), vm((NZ, OWN, D), F32), vm((NZ, OWN, D), BF), vm((NZ, OWN, D), BF),
         vm((2, CH, OWN, 128), BF), vm((CH, 2 * OWN, 128), BF),
         vm((NC * MSG, CH * 2 * OWN), BF), vm((CH * 2 * OWN, NC * MSG), BF),
         vm((CH * GR, GS * MSG), BF), vm((GS * MSG, CH * GR), BF),
@@ -613,9 +666,9 @@
         vm((2, CH, OWN, 128), BF), vm((CH, OWN, 128), BF),
         vm((OM, CH * 2 * OWN), BF), vm((CH * 2 * OWN, OM), BF), vm((OB, NZ * OM), BF), vm((NZ * OM, OB), BF),
         vm((OM, 128), BF), vm((NZ, OM, 128), BF), vm((NX, NY, OB, 128), BF), vm((NX, NY, OB, 128), BF),
-        vm((NX, NY, OB, 128), BF), vm((NY, OB, 128), BF), vm((NY, OB, 128), BF),
+        vm((NY, OB, 128), BF), vm((2, NY, OB, 128), BF), vm((NY, OB, 128), BF), vm((NY, OB, 128), BF),
         vm((NZ, OM, 128), BF), vm((NZ, OM, 128), BF),
-        dma((9,)), dma, dma, dma, dma, dma((NZ - 1,)), dma((NZ - 1,)), dma, dma,
+        dma((9,)), dma, dma, dma, dma, dma((NZ, 2)), dma((NZ, 2)), dma, dma,
         dma((NC,)), dma((NC,)), dma((8, H)), dma((8, H)), dma((OV + NX, H)), dma((OV + NX, H)),
         dma((8, H)), dma((8, H)), dma((NC,)), dma((NC,)), dma, dma,
         dma((NZ,)), dma((NZ,)), dma((NY,)), dma((NY,)), dma((NX, NY)), dma((NX, NY)), dma((NX,)), dma((NX,)),

time: 148 us -> 138 us (0.932); the launches traced: 146 us -> 138 us
  Pallas kernels: 142 us -> 134 us
    pallas_call x1, Pallas kernels: 142 us -> 134 us  [per_device(): pl.pallas_call(kernel, out_shape=(jax.ShapeDtypeStruct((OWN, D), BF), jax...]
where the time goes in v3:
time: 138 us
  Pallas kernels  134 us (97%)
  local copies, waits for them, and re-layouts  3.07 us (2%)
    pallas_call x1, Pallas kernels, per_device(): pl.pallas_call(kernel, out_shape=(jax.ShapeDtypeStruct((OWN, D), BF), jax...  134 us
    unnamed x2, local copies, waits for them, and re-layouts  3.07 us

profile of v3, /device:TPU:1, one launch (start us, length us, event | category | flops | bytes accessed | tf_op | source)
XLA Modules:
  0.0 137.7 jit_solution(1069354313437506532)
XLA Ops:
  0.6 134.0 %shard_map.104 = (bf16[16,2880]{1,0:T(8,128)(2,1)}, bf16[16,2880]{1,0:T(8,128)(2,1)}) custom-call(bf16[128,512]{1,0:T(8,128)(2,1)} %q_hbm.1, bf16[128,128]{1,0:T(8,128)(2,1)} %bitcast.5, bf16[2880,512]{1,0:T(8,128)(2,1)} %bitcast.4, bf16[16,2880]{1,0:T(8,128)(2,1)} %res_hbm.1, f32[2880]{0:T(1024)} %gain_hbm.1, s32[4,128]{1,0:T(4,128)} %bitcast.6, ...), custom_call_target="tpu_custom_call" | custom-call | flops 4000000000 | bytes 8000000 | tf_op jit(solution)/shard_map/pallas_call | solution.py:677
  134.6 1.5 %copy.13 = bf16[16,2880]{1,0:T(8,128)(2,1)} copy(bf16[16,2880]{1,0:T(8,128)(2,1)} %get-tuple-element.4) | data formatting | bytes 184320
  136.2 1.5 %copy.14 = bf16[16,2880]{1,0:T(8,128)(2,1)} copy(bf16[16,2880]{1,0:T(8,128)(2,1)} %get-tuple-element.5) | data formatting | bytes 184320

commit v4 on v3

--- a/solution.py
+++ b/solution.py
@@ -20,7 +20,7 @@
 MSG = 48
 GS, GR = 4, 16
 NR = NC * R
-H = 2
+H = 4
 SB = NR // H
 GH = SB // GR
 FAR = 7
@@ -434,12 +434,12 @@
 
     ox_send(0)
     aside = {
-        (1, 0): (lambda: (ox_send(1), ox_send(7))),
-        (1, 1): (lambda: (ox_send(2), ox_send(6))),
-        (2, 0): (lambda: (ox_send(3), ox_send(5), ox_send(4))),
-        (2, 1): (lambda: ox_take(0)),
-        (3, 0): (lambda: ox_take(3)),
-        (3, 1): (lambda: ox_take(1)),
+        (1, 1): (lambda: (ox_send(1), ox_send(7))),
+        (1, 3): (lambda: (ox_send(2), ox_send(6))),
+        (2, 1): (lambda: (ox_send(3), ox_send(5), ox_send(4))),
+        (2, 3): (lambda: ox_take(0)),
+        (3, 1): (lambda: ox_take(3)),
+        (3, 3): (lambda: ox_take(1)),
     }
     for k in (1, 2, 3):
         for h in range(H):
@@ -453,12 +453,8 @@
                 ag_copy(far_from, FAR, h, far_to).start()
             low(k, h)
             low(k + 3, h)
-            aside[k, h]()
-    loads[7].wait()
-    for h in range(H):
-        ag_copy(far_from, FAR, h, far_to).wait_recv()
-        low(FAR, h)
-
+            if (k, h) in aside:
+                aside[k, h]()
     def expert(slot_at, h):
         lo_copy(slot_at, h).wait_recv()
         inner = low_own[slot_at, rows(h)].astype(F32) + low_oth[slot_at, rows(h)].astype(F32)
@@ -472,18 +468,26 @@
             q_ss.at[slot_at, h], q_rs.at[dst, h], s, head,
         )
 
+    back = tuple(reversed(range(H)))
+    first = 6 - 3 * p
+    first_to = lax.rem(z + 1 + (NZ - 2) * p, NZ)
+    loads[7].wait()
+    for h in back:
+        qs[first, rows(h)] = expert(first, h).astype(BF)
+        q_copy(first, first - 1, h, first_to).start()
     for h in range(H):
+        ag_copy(far_from, FAR, h, far_to).wait_recv()
+        low(FAR, h)
+
+    for h in back:
         qs[FAR, rows(h)] = expert(FAR, h).astype(BF)
         q_copy(FAR, FAR, h, far_back).start()
     ox_take(2)
-    for h in range(H):
-        below, above = expert(3, h), expert(6, h)
+    for h in back:
+        value = expert(far_from, h)
         q_copy(FAR, FAR, h, far_back).wait_recv()
-        got = racc[FAR, rows(h)].astype(F32)
-        qs[3, rows(h)] = (below + jnp.where(p == 0, got, 0.0)).astype(BF)
-        q_copy(3, 2, h, dn).start()
-        qs[6, rows(h)] = (above + jnp.where(p == 0, 0.0, got)).astype(BF)
-        q_copy(6, 5, h, up).start()
+        qs[far_from, rows(h)] = (value + racc[FAR, rows(h)].astype(F32)).astype(BF)
+        q_copy(far_from, far_from - 1, h, far_back).start()
 
     def of_copy(way):
         part = slice(0, 4) if way == 0 else slice(4, 8)
@@ -558,7 +562,7 @@
 
     ov_far()
     for k in (2, 1):
-        for h in range(H):
+        for h in back:
             below, above = expert(k, h), expert(k + 3, h)
             q_copy(k, k, h, dn).wait_recv()
             qs[k, rows(h)] = (below + racc[k, rows(h)].astype(F32)).astype(BF)
@@ -575,7 +579,7 @@
         to = near(r)
         return remote(sb2.at[r], rb2.at[chip], a2_ss.at[r], a2_rs.at[chip], to * 2 + p, z)
 
-    for h in range(H):
+    for h in back:
         value = expert(0, h)
         q_copy(0, 0, h, dn).wait_recv()
         q_copy(0, 3, h, up).wait_recv()
@@ -647,6 +651,17 @@
             if 0 < slot_at < OV:
                 ag_copy(0, slot_at, h, up).wait_send()
                 q_copy(slot_at, slot_at, h, up).wait_send()
+
+
+def deliver(stream_in, esum_in, stream_out, esum_out, sem):
+    copies = [
+        pltpu.make_async_copy(stream_in, stream_out, sem.at[0]),
+        pltpu.make_async_copy(esum_in, esum_out, sem.at[1]),
+    ]
+    for c in copies:
+        c.start()
+    for c in copies:
+        c.wait()
 
 
 def per_device(q, kv, wo, res, gain, ids, weights, w_in, w_out):
@@ -674,7 +689,7 @@
         dma((NZ,)), dma((NZ,)), dma((NY,)), dma((NY,)), dma((NX, NY)), dma((NX, NY)), dma((NX,)), dma((NX,)),
         dma((NY,)), dma((NY,)), dma((NZ,)), dma((NZ,)),
     ]
-    return pl.pallas_call(
+    made = pl.pallas_call(
         kernel,
         out_shape=(jax.ShapeDtypeStruct((OWN, D), BF), jax.ShapeDtypeStruct((OWN, D), BF)),
         in_specs=[pl.BlockSpec(memory_space=pl.ANY)] * 9,
@@ -685,6 +700,13 @@
         ),
         cost_estimate=pl.CostEstimate(flops=4_000_000_000, bytes_accessed=8_000_000, transcendentals=300_000),
     )(q, kv.reshape(TOK, 128), wo.T, res, gain, ids.T, weights.T, w_in, w_out)
+    return pl.pallas_call(
+        deliver,
+        out_shape=(jax.ShapeDtypeStruct((OWN, D), BF), jax.ShapeDtypeStruct((OWN, D), BF)),
+        in_specs=[pl.BlockSpec(memory_space=pl.ANY)] * 2,
+        out_specs=(pl.BlockSpec(memory_space=pl.ANY), pl.BlockSpec(memory_space=pl.ANY)),
+        scratch_shapes=[dma((2,))],
+    )(*made)
 
 
 def solution(mesh):

time: 138 us -> 143 us (1.036)
  Pallas kernels: 134 us -> 142 us
  local copies, waits for them, and re-layouts: 3.07 us -> 0 us
    pallas_call x0 -> x1, Pallas kernels: none -> 6.83 us  [per_device(): pl.pallas_call(deliver, out_shape=(jax.ShapeDtypeStruct((OWN, D), BF), ja...]
    unnamed x2 -> x0, local copies, waits for them, and re-layouts: 3.07 us -> none
where the time goes in v4:
time: 143 us
  Pallas kernels  142 us (99%)
    pallas_call x1, Pallas kernels, per_device(): pl.pallas_call(kernel, out_shape=(jax.ShapeDtypeStruct((OWN, D), BF), jax...  135 us
    pallas_call x1, Pallas kernels, per_device(): pl.pallas_call(deliver, out_shape=(jax.ShapeDtypeStruct((OWN, D), BF), ja...  6.83 us

profile of v4, /device:TPU:1, one launch (start us, length us, event | category | flops | bytes accessed | tf_op | source)
XLA Modules:
  0.0 142.6 jit_solution(18245142717622126374)
XLA Ops:
  0.6 135.0 %shard_map.104 = (bf16[16,2880]{1,0:T(8,128)(2,1)}, bf16[16,2880]{1,0:T(8,128)(2,1)}) custom-call(bf16[128,512]{1,0:T(8,128)(2,1)} %q_hbm.1, bf16[128,128]{1,0:T(8,128)(2,1)} %bitcast.5, bf16[2880,512]{1,0:T(8,128)(2,1)} %bitcast.4, bf16[16,2880]{1,0:T(8,128)(2,1)} %res_hbm.1, f32[2880]{0:T(1024)} %gain_hbm.1, s32[4,128]{1,0:T(4,128)} %bitcast.6, ...), custom_call_target="tpu_custom_call" | custom-call | flops 4000000000 | bytes 8000000 | tf_op jit(solution)/shard_map/pallas_call | solution.py:692
  135.6 6.8 %shard_map.105 = (bf16[16,2880]{1,0:T(8,128)(2,1)}, bf16[16,2880]{1,0:T(8,128)(2,1)}) custom-call(bf16[16,2880]{1,0:T(8,128)(2,1)} %get-tuple-element.4.stream_in, bf16[16,2880]{1,0:T(8,128)(2,1)} %get-tuple-element.5.esum_in), custom_call_target="tpu_custom_call" | custom-call | tf_op jit(solution)/shard_map/pallas_call | solution.py:703

commit v5 on v3

--- a/solution.py
+++ b/solution.py
@@ -26,7 +26,8 @@
 FAR = 7
 OV = 8
 OM = 32
-PIECES = ((0, 1536), (1536, D))
+PIECES = ((0, 1024), (1024, 2048), (2048, D))
+NP = len(PIECES)
 OB = CH * OWN
 
 NEAR = sorted(
@@ -233,7 +234,7 @@
     ra = iota((NC * R, 128), 0)
     expand = ones(idiv(ra, R) == iota((NC * R, 128), 1))
 
-    for c in range(2):
+    for c in range(NP):
         got = got_h(FAR, c)
         send_h(3, 2, c, dn, block(-3, c) + jnp.where(p == 0, got, 0.0))
         send_h(6, 5, c, up, block(3, c) + jnp.where(p == 0, 0.0, got))
@@ -259,7 +260,7 @@
     dm[...] = full.reshape(NC * MSG, CH * 2 * OWN).astype(BF)
 
 
-    for c in range(2):
+    for c in range(NP):
         send_h(2, 1, c, dn, block(-2, c) + got_h(2, c))
         send_h(5, 4, c, up, block(2, c) + got_h(5, c))
 
@@ -275,13 +276,13 @@
     hot_y = jnp.sum(hot * idiv(e_row, NX).astype(F32), axis=1, keepdims=True)
 
 
-    for c in range(2):
+    for c in range(NP):
         send_h(1, 0, c, dn, block(-1, c) + got_h(1, c))
         send_h(4, 3, c, up, block(1, c) + got_h(4, c))
 
     loads[4].wait()
     loads[5].wait()
-    total = jnp.concatenate([block(0, c) + (got_h(0, c) + got_h(3, c)) for c in range(2)], axis=1)
+    total = jnp.concatenate([block(0, c) + (got_h(0, c) + got_h(3, c)) for c in range(NP)], axis=1)
     total = total + res_v[...].astype(F32)
     stream_ref[...] = total.astype(BF)
     mean_square = jnp.mean(total * total, axis=-1, keepdims=True)
@@ -628,7 +629,7 @@
         oy_copy(d).wait_send()
         oyr_copy(d).wait_send()
         ozr_copy(d).wait_send()
-        for c in range(2):
+        for c in range(NP):
             h_copy(d, d, c, up).wait_send()
     for way in range(2):
         of_copy(way).wait_send()
@@ -647,6 +648,11 @@
             if 0 < slot_at < OV:
                 ag_copy(0, slot_at, h, up).wait_send()
                 q_copy(slot_at, slot_at, h, up).wait_send()
+
+
+def deliver(stream_in, esum_in, stream_out, esum_out):
+    stream_out[...] = stream_in[...]
+    esum_out[...] = esum_in[...]
 
 
 def per_device(q, kv, wo, res, gain, ids, weights, w_in, w_out):
@@ -668,13 +674,13 @@
         vm((OM, 128), BF), vm((NZ, OM, 128), BF), vm((NX, NY, OB, 128), BF), vm((NX, NY, OB, 128), BF),
         vm((NY, OB, 128), BF), vm((2, NY, OB, 128), BF), vm((NY, OB, 128), BF), vm((NY, OB, 128), BF),
         vm((NZ, OM, 128), BF), vm((NZ, OM, 128), BF),
-        dma((9,)), dma, dma, dma, dma, dma((NZ, 2)), dma((NZ, 2)), dma, dma,
+        dma((9,)), dma, dma, dma, dma, dma((NZ, NP)), dma((NZ, NP)), dma, dma,
         dma((NC,)), dma((NC,)), dma((8, H)), dma((8, H)), dma((OV + NX, H)), dma((OV + NX, H)),
         dma((8, H)), dma((8, H)), dma((NC,)), dma((NC,)), dma, dma,
         dma((NZ,)), dma((NZ,)), dma((NY,)), dma((NY,)), dma((NX, NY)), dma((NX, NY)), dma((NX,)), dma((NX,)),
         dma((NY,)), dma((NY,)), dma((NZ,)), dma((NZ,)),
     ]
-    return pl.pallas_call(
+    made = pl.pallas_call(
         kernel,
         out_shape=(jax.ShapeDtypeStruct((OWN, D), BF), jax.ShapeDtypeStruct((OWN, D), BF)),
         in_specs=[pl.BlockSpec(memory_space=pl.ANY)] * 9,
@@ -685,6 +691,12 @@
         ),
         cost_estimate=pl.CostEstimate(flops=4_000_000_000, bytes_accessed=8_000_000, transcendentals=300_000),
     )(q, kv.reshape(TOK, 128), wo.T, res, gain, ids.T, weights.T, w_in, w_out)
+    return pl.pallas_call(
+        deliver,
+        out_shape=(jax.ShapeDtypeStruct((OWN, D), BF), jax.ShapeDtypeStruct((OWN, D), BF)),
+        in_specs=[pl.BlockSpec(memory_space=vm)] * 2,
+        out_specs=(pl.BlockSpec(memory_space=vm), pl.BlockSpec(memory_space=vm)),
+    )(*made)
 
 
 def solution(mesh):

time: 138 us -> 135 us (0.978)
  local copies, waits for them, and re-layouts: 3.07 us -> 0 us
    unnamed x2 -> x0, local copies, waits for them, and re-layouts: 3.07 us -> none
    pallas_call x0 -> x1, Pallas kernels: none -> 1.62 us  [per_device(): pl.pallas_call(deliver, out_shape=(jax.ShapeDtypeStruct((OWN, D), BF), ja...]
where the time goes in v5:
time: 135 us
  Pallas kernels  134 us (99%)
    pallas_call x1, Pallas kernels, per_device(): pl.pallas_call(kernel, out_shape=(jax.ShapeDtypeStruct((OWN, D), BF), jax...  133 us

profile of v5, /device:TPU:1, one launch (start us, length us, event | category | flops | bytes accessed | tf_op | source)
XLA Modules:
  0.0 135.0 jit_solution(1469705110125207304)
XLA Ops:
  0.6 132.8 %shard_map.104 = (bf16[16,2880]{1,0:T(8,128)(2,1)}, bf16[16,2880]{1,0:T(8,128)(2,1)}) custom-call(bf16[128,512]{1,0:T(8,128)(2,1)} %q_hbm.1, bf16[128,128]{1,0:T(8,128)(2,1)} %bitcast.5, bf16[2880,512]{1,0:T(8,128)(2,1)} %bitcast.4, bf16[16,2880]{1,0:T(8,128)(2,1)} %res_hbm.1, f32[2880]{0:T(1024)} %gain_hbm.1, s32[4,128]{1,0:T(4,128)} %bitcast.6, ...), custom_call_target="tpu_custom_call" | custom-call | flops 4000000000 | bytes 8000000 | tf_op jit(solution)/shard_map/pallas_call | solution.py:683
  133.4 1.6 %shard_map.105 = (bf16[16,2880]{1,0:T(8,128)(2,1)}, bf16[16,2880]{1,0:T(8,128)(2,1)}) custom-call(bf16[16,2880]{1,0:T(8,128)(2,1)} %get-tuple-element.4.stream_in, bf16[16,2880]{1,0:T(8,128)(2,1)} %get-tuple-element.5.esum_in), custom_call_target="tpu_custom_call" | custom-call | tf_op jit(solution)/shard_map/pallas_call | solution.py:694

commit v6 on v5

--- a/solution.py
+++ b/solution.py
@@ -24,6 +24,9 @@
 SB = NR // H
 GH = SB // GR
 FAR = 7
+WHOLE = HALF // 128
+TAIL = WHOLE * SB
+PACK = TAIL + SB // 4
 OV = 8
 OM = 32
 PIECES = ((0, 1024), (1024, 2048), (2048, D))
@@ -60,6 +63,19 @@
 
 def ones(cond):
     return jnp.where(cond, 1.0, 0.0).astype(BF)
+
+
+def pack(value):
+    part = SB // 4
+    last = [value[part * j:part * (j + 1), 128 * WHOLE:] for j in range(4)]
+    whole = [value[:, 128 * c:128 * (c + 1)] for c in range(WHOLE)]
+    return jnp.concatenate(whole + [jnp.concatenate(last, axis=1)], axis=0)
+
+
+def unpack(packed):
+    last = [packed[TAIL:, 32 * j:32 * (j + 1)] for j in range(4)]
+    whole = [packed[SB * c:SB * (c + 1)] for c in range(WHOLE)]
+    return jnp.concatenate(whole + [jnp.concatenate(last, axis=0)], axis=1)
 
 
 def kernel(
@@ -360,7 +376,7 @@
 
     def ag_copy(src, dst, h, head):
         return remote(
-            slots.at[src, rows(h)], slots.at[dst, rows(h)],
+            slots.at[src, h], slots.at[dst, h],
             ag_ss.at[dst, h], ag_rs.at[dst, h], s, head,
         )
 
@@ -371,7 +387,7 @@
         )
 
     def low(slot_at, h):
-        low_own[slot_at, rows(h)] = dot(slots[slot_at, rows(h)], win_v[...]).astype(BF)
+        low_own[slot_at, rows(h)] = dot(unpack(slots[slot_at, h]), win_v[...]).astype(BF)
         lo_copy(slot_at, h).start()
 
     for h in range(H):
@@ -379,9 +395,10 @@
             for i in range(GS):
                 a1_wait(g * GS + i)
             got = dot(pm[...], rb1[GS * g:GS * (g + 1)].reshape(GS * MSG, 128)).astype(BF)
-            for c in range(CH):
-                width = min(128, HALF - 128 * c)
-                slots[0, GR * g:GR * (g + 1), 128 * c:128 * c + width] = got[GR * c:GR * (c + 1), :width]
+            i = g - h * GH
+            for c in range(WHOLE):
+                slots[0, h, SB * c + GR * i:SB * c + GR * (i + 1)] = got[GR * c:GR * (c + 1)]
+            slots[0, h, TAIL:, 32 * i:32 * (i + 1)] = got[GR * WHOLE:, :32]
         ag_copy(0, 1, h, up).start()
         ag_copy(0, 4, h, dn).start()
     for d in range(1, NZ):
@@ -426,11 +443,12 @@
                     ox_copy(2, left, from_y).start()
                 if d == 1 and from_y >= 4:
                     ox_copy(3, right, from_y).start()
-        for c in range(CH):
-            width = min(128, HALF - 128 * c)
-            piece = ox[from_x, :, OWN * c:OWN * (c + 1), :].reshape(NR, 128)
-            slots[OV + d, :, 128 * c:128 * c + width] = piece[:, :width]
         for h in range(H):
+            for c in range(WHOLE):
+                piece = ox[from_x, 4 * h:4 * (h + 1), OWN * c:OWN * (c + 1), :]
+                slots[OV + d, h, SB * c:SB * (c + 1)] = piece.reshape(SB, 128)
+            for j in range(4):
+                slots[OV + d, h, TAIL:, 32 * j:32 * (j + 1)] = ox[from_x, 4 * h + j, OWN * WHOLE:, :][:, :32]
             low(OV + d, h)
 
     ox_send(0)
@@ -465,25 +483,25 @@
         inner = low_own[slot_at, rows(h)].astype(F32) + low_oth[slot_at, rows(h)].astype(F32)
         gate, upv = inner[:, :192], inner[:, 192:]
         active = ((upv + 1.0) * gate * jax.nn.sigmoid(1.702 * gate)).astype(BF)
-        return dot(active, wout_v[...])
+        return pack(dot(active, wout_v[...]))
 
     def q_copy(slot_at, dst, h, head):
         return remote(
-            qs.at[slot_at, rows(h)], racc.at[dst, rows(h)],
+            qs.at[slot_at, h], racc.at[dst, h],
             q_ss.at[slot_at, h], q_rs.at[dst, h], s, head,
         )
 
     for h in range(H):
-        qs[FAR, rows(h)] = expert(FAR, h).astype(BF)
+        qs[FAR, h] = expert(FAR, h).astype(BF)
         q_copy(FAR, FAR, h, far_back).start()
     ox_take(2)
     for h in range(H):
         below, above = expert(3, h), expert(6, h)
         q_copy(FAR, FAR, h, far_back).wait_recv()
-        got = racc[FAR, rows(h)].astype(F32)
-        qs[3, rows(h)] = (below + jnp.where(p == 0, got, 0.0)).astype(BF)
+        got = racc[FAR, h].astype(F32)
+        qs[3, h] = (below + jnp.where(p == 0, got, 0.0)).astype(BF)
         q_copy(3, 2, h, dn).start()
-        qs[6, rows(h)] = (above + jnp.where(p == 0, 0.0, got)).astype(BF)
+        qs[6, h] = (above + jnp.where(p == 0, 0.0, got)).astype(BF)
         q_copy(6, 5, h, up).start()
 
     def of_copy(way):
@@ -511,12 +529,12 @@
     def ov_expert(d):
         for h in range(H):
             value = expert(OV + d, h).astype(BF)
-            n = SB // OWN
-            for c in range(CH):
-                piece = value[:, 128 * c:128 * (c + 1)]
-                if piece.shape[1] < 128:
-                    piece = jnp.concatenate([piece, jnp.zeros((SB, 128 * CH - HALF), BF)], axis=1)
-                obuf[d, n * h:n * (h + 1), OWN * c:OWN * (c + 1), :] = piece.reshape(n, OWN, 128)
+            for c in range(WHOLE):
+                piece = value[SB * c:SB * (c + 1)]
+                obuf[d, 4 * h:4 * (h + 1), OWN * c:OWN * (c + 1), :] = piece.reshape(4, OWN, 128)
+            for j in range(4):
+                last = [value[TAIL:, 32 * j:32 * (j + 1)], jnp.zeros((OWN, 96), BF)]
+                obuf[d, 4 * h + j, OWN * WHOLE:, :] = jnp.concatenate(last, axis=1)
 
     def ov_far():
         ov_expert(2)
@@ -562,10 +580,10 @@
         for h in range(H):
             below, above = expert(k, h), expert(k + 3, h)
             q_copy(k, k, h, dn).wait_recv()
-            qs[k, rows(h)] = (below + racc[k, rows(h)].astype(F32)).astype(BF)
+            qs[k, h] = (below + racc[k, h].astype(F32)).astype(BF)
             q_copy(k, k - 1, h, dn).start()
             q_copy(k + 3, k + 3, h, up).wait_recv()
-            qs[k + 3, rows(h)] = (above + racc[k + 3, rows(h)].astype(F32)).astype(BF)
+            qs[k + 3, h] = (above + racc[k + 3, h].astype(F32)).astype(BF)
             q_copy(k + 3, k + 2, h, up).start()
         if k == 2:
             ov_near()
@@ -580,12 +598,11 @@
         value = expert(0, h)
         q_copy(0, 0, h, dn).wait_recv()
         q_copy(0, 3, h, up).wait_recv()
-        value = (value + racc[0, rows(h)].astype(F32) + racc[3, rows(h)].astype(F32)).astype(BF)
+        value = (value + racc[0, h].astype(F32) + racc[3, h].astype(F32)).astype(BF)
         for i in range(GH):
             g = h * GH + i
-            part = value[GR * i:GR * (i + 1)]
-            pieces = [part[:, 128 * c:128 * (c + 1)] for c in range(CH - 1)]
-            last = part[:, 128 * (CH - 1):]
+            pieces = [value[SB * c + GR * i:SB * c + GR * (i + 1)] for c in range(WHOLE)]
+            last = value[TAIL:, 32 * i:32 * (i + 1)]
             pieces.append(jnp.concatenate([last, jnp.zeros((GR, 128 * CH - HALF), BF)], axis=1))
             out = dot(pt[...], jnp.concatenate(pieces, axis=0)).astype(BF)
             sb2[GS * g:GS * (g + 1)] = out.reshape(GS, MSG, 128)
@@ -666,8 +683,8 @@
         vm((NC * MSG, CH * 2 * OWN), BF), vm((CH * 2 * OWN, NC * MSG), BF),
         vm((CH * GR, GS * MSG), BF), vm((GS * MSG, CH * GR), BF),
         vm((NC, MSG, 128), BF), vm((NC, MSG, 128), BF),
-        vm((OV + NX, NR, HALF), BF), vm((OV + NX, NR, 384), BF), vm((OV + NX, NR, 384), BF),
-        vm((8, NR, HALF), BF), vm((8, NR, HALF), BF),
+        vm((OV + NX, H, PACK, 128), BF), vm((OV + NX, NR, 384), BF), vm((OV + NX, NR, 384), BF),
+        vm((8, H, PACK, 128), BF), vm((8, H, PACK, 128), BF),
         vm((NC, MSG, 128), BF), vm((NC, MSG, 128), BF),
         vm((2, CH, OWN, 128), BF), vm((CH, OWN, 128), BF),
         vm((OM, CH * 2 * OWN), BF), vm((CH * 2 * OWN, OM), BF), vm((OB, NZ * OM), BF), vm((NZ * OM, OB), BF),

time: 135 us -> 134 us (level)
  no operation moved by 1% of the time
where the time goes in v6:
time: 134 us
  Pallas kernels  133 us (99%)
    pallas_call x1, Pallas kernels, per_device(): pl.pallas_call(kernel, out_shape=(jax.ShapeDtypeStruct((OWN, D), BF), jax...  132 us

profile of v6, /device:TPU:1, one launch (start us, length us, event | category | flops | bytes accessed | tf_op | source)
XLA Modules:
  0.0 134.1 jit_solution(16656332334397967667)
XLA Ops:
  0.6 131.8 %shard_map.104 = (bf16[16,2880]{1,0:T(8,128)(2,1)}, bf16[16,2880]{1,0:T(8,128)(2,1)}) custom-call(bf16[128,512]{1,0:T(8,128)(2,1)} %q_hbm.1, bf16[128,128]{1,0:T(8,128)(2,1)} %bitcast.5, bf16[2880,512]{1,0:T(8,128)(2,1)} %bitcast.4, bf16[16,2880]{1,0:T(8,128)(2,1)} %res_hbm.1, f32[2880]{0:T(1024)} %gain_hbm.1, s32[4,128]{1,0:T(4,128)} %bitcast.6, ...), custom_call_target="tpu_custom_call" | custom-call | flops 4000000000 | bytes 8000000 | tf_op jit(solution)/shard_map/pallas_call | solution.py:700
  132.5 1.6 %shard_map.105 = (bf16[16,2880]{1,0:T(8,128)(2,1)}, bf16[16,2880]{1,0:T(8,128)(2,1)}) custom-call(bf16[16,2880]{1,0:T(8,128)(2,1)} %get-tuple-element.4.stream_in, bf16[16,2880]{1,0:T(8,128)(2,1)} %get-tuple-element.5.esum_in), custom_call_target="tpu_custom_call" | custom-call | tf_op jit(solution)/shard_map/pallas_call | solution.py:711
